TPU v7x, 32 devices: a whole 2x2x4 slice. The times are simulated.
32 devices in a mesh: inst: 8 (over y, x, core), tp: 4 (over z).
Axes of the slice: x: 2, y: 2, z: 4, core: 2. Of those that a mesh axis runs over, the one named last changes fastest.
Arguments:
- hidden: bfloat16 [4, 256, 8192], P(None, 'inst'), may hold values from -6 to 6
- query_weight: bfloat16 [8192, 2048], P(None, 'tp'), may hold values from -0.0625 to 0.0625
- output_weight: bfloat16 [2048, 8192], P('tp'), may hold values from -0.125 to 0.125
- kv_pool: bfloat16 [768, 2, 64, 512], P('inst', None, None, 'tp'), may hold values from -620 to 620
- new_kv: bfloat16 [4, 256, 2, 512], P(None, 'inst', None, 'tp'), may hold values from -6 to 6
- lengths: int32 [256], P('inst'), may hold values from 1 to 192, as said below
- page_table: int32 [256, 3], P('inst'), may hold values from 0 to 95, as said below
- mig_req: int32 [64], P('inst'), may hold values from 0 to 31, as said below
- mig_dest: int32 [64, 1], P('inst'), may hold values from 0 to 7; in each aligned block of 8 rows (0 to 7, 8 to 15, ...) at most 2 rows name the same one
- resume: int32 [64], P('inst'), may hold values from 0 to 3
Outputs:
- home_out: bfloat16 [4, 256, 8192], P(None, 'inst', 'tp')
- arrival_out: bfloat16 [4, 128, 8192], P(None, 'inst', 'tp')
- arrival_cache: bfloat16 [128, 3, 2, 64, 512], P('inst', None, None, None, 'tp')
Inputs may be any that keep to these rules, and one draw needn't show every extreme that they name: Every draw has a request with exactly 192 cached tokens; typical lengths differ between instances by up to a factor of four. `page_table`: each instance's rows together name every page number of its pool exactly once. `mig_req`: the leaving requests of one instance are distinct. `mig_dest`: among the rows of one instance, no instance is named more than 2 times.
All inputs are finite; a program needn't handle non-finite values.
Results may differ from a plain program's by a relative error of at most 0.012.
Values may be sent and summed in bfloat16 or wider, within the bound.
A program may use at most 128 MiB of HBM per device.

v0:
```python
import jax
import jax.numpy as jnp
from jax import lax
from jax.sharding import PartitionSpec as P

HD = 128
GROUP = 4
CAP = 2


ROPE_BASE = 500000.0


def rotate(query, position):
    half = query.shape[-1] // 2
    inverse = ROPE_BASE ** (-jnp.arange(half, dtype=jnp.float32) * 2.0 / query.shape[-1])
    angles = position.astype(jnp.float32)[..., None] * inverse
    angles = jnp.concatenate([angles, angles], axis=-1)
    turned = jnp.concatenate([-query[..., half:], query[..., :half]], axis=-1)
    return query * jnp.cos(angles) + turned * jnp.sin(angles)


def attend(query, pages, length, fresh):
    count = pages.shape[0]
    depth = query.shape[-1]
    steps_n = query.shape[0]
    keys = pages[:, :, 0].reshape(count, -1, depth)
    values = pages[:, :, 1].reshape(count, -1, depth)
    scale = depth ** (-0.5)
    older = jnp.einsum("sbgd,bld->bsgl", query, keys, preferred_element_type=jnp.float32) * scale
    newer = (
        jnp.einsum("sbgd,ubd->bsgu", query, fresh[:, :, 0], preferred_element_type=jnp.float32)
        * scale
    )
    live = jnp.arange(keys.shape[1], dtype=jnp.int32)[None, :] < length[:, None]
    older = jnp.where(live[:, None, None, :], older, -1e30)
    step_ids = jnp.arange(steps_n, dtype=jnp.int32)
    causal = step_ids[None, :] <= step_ids[:, None]
    newer = jnp.where(causal[None, :, None, :], newer, -1e30)
    top = jnp.maximum(jnp.max(older, axis=-1), jnp.max(newer, axis=-1))[..., None]
    older_w = jnp.exp(older - top)
    newer_w = jnp.exp(newer - top)
    total = (jnp.sum(older_w, axis=-1) + jnp.sum(newer_w, axis=-1))[..., None]
    older_p = (older_w / total).astype(jnp.bfloat16)
    newer_p = (newer_w / total).astype(jnp.bfloat16)
    result = jnp.einsum("bsgl,bld->sbgd", older_p, values, preferred_element_type=jnp.float32)
    result = result + jnp.einsum(
        "bsgu,ubd->sbgd", newer_p, fresh[:, :, 1], preferred_element_type=jnp.float32
    )
    return result.astype(jnp.bfloat16).reshape(steps_n, count, -1)


def local(
    hidden,
    query_weight,
    output_weight,
    kv_pool,
    new_kv,
    lengths,
    page_table,
    mig_req,
    mig_dest,
    resume,
):
    steps_n, local_rows, width = hidden.shape
    instances = lax.axis_size("inst")
    query = jnp.dot(hidden.reshape(-1, width), query_weight, preferred_element_type=jnp.float32)
    query = query.reshape(steps_n, local_rows, GROUP, HD)
    position = lengths[None, :] + jnp.arange(steps_n, dtype=jnp.int32)[:, None]
    rotated = rotate(query, position[:, :, None]).astype(jnp.bfloat16)
    pages = kv_pool[page_table]
    attended = attend(rotated, pages, lengths, new_kv)
    leaving = mig_req.shape[0]
    order = jnp.arange(leaving, dtype=jnp.int32)
    hit = mig_req[:, None] == jnp.arange(local_rows, dtype=jnp.int32)[None, :]
    moved = jnp.min(jnp.where(hit, resume[:, None], steps_n), axis=0)
    step_ids = jnp.arange(steps_n, dtype=jnp.int32)[:, None]
    home_rows = jnp.where(
        (step_ids < moved[None, :])[:, :, None], attended, jnp.zeros_like(attended)
    )
    dest = mig_dest[:, 0]
    same = dest[None, :] == dest[:, None]
    earlier = order[None, :] < order[:, None]
    rank = jnp.sum((same & earlier).astype(jnp.int32), axis=1)
    slot = dest * CAP + rank
    slot_ids = jnp.arange(instances * CAP, dtype=jnp.int32)
    chosen = (slot_ids[:, None] == slot[None, :]).astype(jnp.int32)
    slot_request = jnp.sum(chosen * mig_req[None, :], axis=1)
    filled = jnp.sum(chosen, axis=1)
    slot_resume = jnp.where(filled > 0, jnp.sum(chosen * resume[None, :], axis=1), steps_n)
    slot_pages = jnp.where(
        (filled > 0)[:, None, None, None, None], pages[slot_request], jnp.zeros_like(pages[:1])
    )
    slot_query = jnp.transpose(rotated[:, slot_request], (1, 0, 2, 3)).reshape(
        instances * CAP, steps_n, GROUP * HD
    )
    slot_fresh = jnp.transpose(new_kv[:, slot_request], (1, 0, 2, 3))
    got_pages, got_query, got_fresh = (
        lax.all_to_all(slot_pages, "inst", split_axis=0, concat_axis=0, tiled=True),
        lax.all_to_all(slot_query, "inst", split_axis=0, concat_axis=0, tiled=True),
        lax.all_to_all(slot_fresh, "inst", split_axis=0, concat_axis=0, tiled=True),
    )
    slot_meta = jnp.stack([lengths[slot_request], slot_resume], axis=1)
    got_meta = lax.all_to_all(slot_meta, "inst", split_axis=0, concat_axis=0, tiled=True)
    arrive_query = jnp.transpose(
        got_query.reshape(instances * CAP, steps_n, GROUP, HD), (1, 0, 2, 3)
    )
    arrive_fresh = jnp.transpose(got_fresh, (1, 0, 2, 3))
    arrived = attend(arrive_query, got_pages, got_meta[:, 0], arrive_fresh)
    arrival_rows = jnp.where(
        (step_ids >= got_meta[None, :, 1])[:, :, None], arrived, jnp.zeros_like(arrived)
    )
    combined = jnp.concatenate([home_rows, arrival_rows], axis=1)
    partial_sum = jnp.dot(
        combined.reshape(-1, combined.shape[-1]), output_weight, preferred_element_type=jnp.float32
    )
    partial_sum = partial_sum.reshape(steps_n, -1, width)
    summed = lax.psum(partial_sum, "tp")
    share = width // lax.axis_size("tp")
    mine = lax.dynamic_slice_in_dim(summed, lax.axis_index("tp") * share, share, 2)
    mine = mine.astype(jnp.bfloat16)
    return (mine[:, :local_rows], mine[:, local_rows:], got_pages)


def solution(mesh):
    in_specs = (
        P(None, "inst", None),
        P(None, "tp"),
        P("tp", None),
        P("inst", None, None, "tp"),
        P(None, "inst", None, "tp"),
        P("inst"),
        P("inst", None),
        P("inst"),
        P("inst", None),
        P("inst"),
    )
    out_specs = (P(None, "inst", "tp"), P(None, "inst", "tp"), P("inst", None, None, None, "tp"))
    return jax.shard_map(local, mesh=mesh, in_specs=in_specs, out_specs=out_specs, check_vma=False)
```

profile of v0, /device:TPU:0, one launch (start us, length us, event | category | flops | bytes accessed | tf_op | source)
XLA Modules:
  0.0 330.6 jit_solution(5007286926806465190)
XLA Ops:
  0.6 1.0 convert_reduce_fusion.1
  1.6 0.7 multiply_add_fusion
  2.3 0.8 select_reduce_fusion
  3.1 1.3 gather_fusion.1
  4.5 0.1 select_n.73
  4.6 0.6 copy.128
  5.2 5.2 %all-to-all-start = ((s32[8,2,2]{1,2,0:T(2,128)}), s32[8,2,2]{1,2,0:T(2,128)S(1)}, u32[]{:S(2)}, u32[]{:S(2)}) async-start(s32[8,2,2]{1,2,0:T(2,128)} %copy.128), calls=%async_computation | async-start | bytes 16384 | tf_op jit(solution)/shard_map/all_to_all | solution.py:104
  10.4 0.7 add_convert_fusion
  11.0 0.7 iota_compare_fusion
  11.8 0.7 compare_select_fusion
  12.5 0.1 copy.115
  12.6 0.1 reshape.261
  12.7 2.7 gather_fusion
  15.4 4.4 %fusion.36 = (bf16[32,3,1,64,128]{4,3,2,1,0:T(8,128)(2,1)}, bf16[32,3,1,64,128]{4,3,2,1,0:T(8,128)(2,1)}) fusion(bf16[32,3,2,64,128]{4,3,2,1,0:T(8,128)(2,1)} %bitcast.103), kind=kLoop, calls=%fused_computation.94 | loop fusion | bytes 6291456 | tf_op jit(solution)/shard_map/slice | solution.py:27
  19.8 3.8 %gather_fusion.2 = bf16[16,3,2,64,128]{4,3,2,1,0:T(8,128)(2,1)} fusion(bf16[32,3,2,64,128]{4,3,2,1,0:T(8,128)(2,1)} %bitcast.104, s32[1024]{0:T(1024)S(1)} %pad_clamp_fusion), kind=kCustom, calls=%fused_computation.2 | custom fusion | bytes 3145792 | tf_op jit(solution)/shard_map/gather | solution.py:92
  23.6 11.4 %copy.147 = bf16[512,8192]{1,0:T(8,128)(2,1)} copy(bf16[512,8192]{0,1:T(8,128)(2,1)} %bitcast.105) | data formatting | bytes 16777216 | tf_op jit(solution)/shard_map/dot_general | solution.py:67
  35.0 7.0 %fusion.2 = f32[4,32,4,128]{3,1,2,0:T(8,128)S(1)} fusion(bf16[4,128,8192,1]{2,1,0,3:T(8,128)(2,1)} %bitcast.106, bf16[4,32,8192]{2,1,0:T(8,128)(2,1)} %param.10), kind=kOutput, calls=%fused_computation.7 | convolution fusion | flops 1073741824 | bytes 10747904 | tf_op jit(solution)/shard_map/dot_general | solution.py:67
  42.0 0.1 slice_negate_fusion
  42.2 0.3 fusion.30
  42.5 0.7 fusion.38
  43.2 0.1 fusion.13
  43.4 2.0 fusion.23
  45.3 1.1 copy.120
  46.5 0.1 fusion.31
  46.6 0.1 copy.121
  46.7 3.2 fusion.41
  49.9 0.1 copy.122
  50.0 0.1 fusion.32
  50.1 0.7 copy.123
  50.9 1.4 fusion.11
  52.3 0.9 add.76
  53.2 0.1 copy.124
  53.3 2.9 convolution_bitcast_fusion.1
  56.2 1.3 broadcast_select_fusion
  57.5 0.6 gather_fusion.4
  58.2 0.6 copy.133
  58.8 4.2 %all-to-all-start.3 = ((bf16[16,4,2,128]{3,1,2,0:T(4,128)(2,1)}), bf16[16,4,2,128]{3,1,2,0:T(4,128)(2,1)S(1)}, u32[]{:S(2)}, u32[]{:S(2)}) async-start(bf16[16,4,2,128]{3,1,2,0:T(4,128)(2,1)} %copy.133), calls=%async_computation.3 | async-start | bytes 65536 | tf_op jit(solution)/shard_map/all_to_all | solution.py:101
  63.0 0.1 divide_convert_fusion.6
  63.2 0.9 copy.126
  64.0 0.6 gather_fusion.3
  64.7 0.7 reshape.312
  65.3 2.5 all-to-all-done.3
  67.8 3.3 %all-to-all-start.2 = ((bf16[16,4,512]{2,1,0:T(4,128)(2,1)}), bf16[16,4,512]{2,1,0:T(4,128)(2,1)S(1)}, u32[]{:S(2)}, u32[]{:S(2)}) async-start(bf16[16,4,512]{2,1,0:T(4,128)(2,1)} %reshape.312), calls=%async_computation.2 | async-start | bytes 131072 | tf_op jit(solution)/shard_map/all_to_all | solution.py:100
  71.2 1.2 fusion.7
  72.4 3.7 %all-to-all-done.2 = bf16[16,4,512]{2,1,0:T(4,128)(2,1)S(1)} async-done(((bf16[16,4,512]{2,1,0:T(4,128)(2,1)}), bf16[16,4,512]{2,1,0:T(4,128)(2,1)S(1)}, u32[]{:S(2)}, u32[]{:S(2)}) %all-to-all-start.2) | async-done | bytes 65568 | tf_op jit(solution)/shard_map/all_to_all | solution.py:100
  76.1 4.5 %all-to-all-start.1 = ((bf16[16,3,2,64,128]{4,3,2,1,0:T(8,128)(2,1)}), bf16[16,3,2,64,128]{4,3,2,1,0:T(8,128)(2,1)}, u32[]{:S(2)}, u32[]{:S(2)}) async-start(bf16[16,3,2,64,128]{4,3,2,1,0:T(8,128)(2,1)} %broadcast_select_fusion), calls=%async_computation.1 | async-start | bytes 3145728 | tf_op jit(solution)/shard_map/all_to_all | solution.py:99
  80.6 0.1 select_reduce_fusion.2
  80.8 0.1 copy_select_fusion
  80.9 0.1 all_to_all.16
  81.1 0.7 fusion.40
  81.8 19.6 %all-to-all-done.1 = bf16[16,3,2,64,128]{4,3,2,1,0:T(8,128)(2,1)} async-done(((bf16[16,3,2,64,128]{4,3,2,1,0:T(8,128)(2,1)}), bf16[16,3,2,64,128]{4,3,2,1,0:T(8,128)(2,1)}, u32[]{:S(2)}, u32[]{:S(2)}) %all-to-all-start.1) | async-done | bytes 1572896 | tf_op jit(solution)/shard_map/all_to_all | solution.py:99
  101.5 1.5 fusion.37
  103.0 0.6 fusion.39
  103.6 0.3 fusion.16
  103.9 0.1 fusion.22
  104.1 0.3 fusion.28
  104.3 0.4 fusion.10
  104.8 0.1 copy_select_fusion.1
  104.9 7.9 %fusion = f32[4,48,8192]{2,1,0:T(8,128)} fusion(bf16[512,8192]{1,0:T(8,128)(2,1)} %param.12, bf16[4,16,512]{2,1,0:T(8,128)(2,1)S(1)} %copy_select_fusion.1, bf16[4,32,512]{2,1,0:T(8,128)(2,1)S(1)} %copy_select_fusion), kind=kOutput, calls=%fused_computation.5 | convolution fusion | flops 1611005952 | bytes 14876672 | tf_op jit(solution)/shard_map/dot_general | solution.py:114
  112.7 212.3 %all-reduce.1 = bf16[4,48,8192]{2,1,0:T(8,128)(2,1)} all-reduce(f32[4,48,8192]{2,1,0:T(8,128)} %fusion), channel_id=1, replica_groups=mesh['inst'=8,'tp'=4] {'tp'}, use_global_device_ids=true, to_apply=%region_13.14 | all-reduce | flops 1572864 | bytes 9437184 | tf_op jit(solution)/shard_map/psum | solution.py:118
  325.0 1.2 dynamic-slice_convert_fusion
  326.2 0.8 slice.74
  327.1 0.7 slice.75
  327.8 2.8 copy.168
  (34 shorter events, 0.6 us)
Async XLA Ops:
  0.6 12.0 %copy-start = (bf16[96,2,64,128]{3,2,1,0:T(8,128)(2,1)S(1)}, bf16[96,2,64,128]{3,2,1,0:T(8,128)(2,1)}, u32[]{:S(2)}) copy-start(bf16[96,2,64,128]{3,2,1,0:T(8,128)(2,1)} %param.13) | copy-start | bytes 9437188
  5.2 53.6 %all-to-all-start = ((s32[8,2,2]{1,2,0:T(2,128)}), s32[8,2,2]{1,2,0:T(2,128)S(1)}, u32[]{:S(2)}, u32[]{:S(2)}) async-start(s32[8,2,2]{1,2,0:T(2,128)} %copy.128), calls=%async_computation | async-start | bytes 16384 | tf_op jit(solution)/shard_map/all_to_all | solution.py:104
  35.0 7.5 %copy-start.2 = (bf16[4,32,2,128]{3,2,1,0:T(2,128)(2,1)S(1)}, bf16[4,32,2,128]{3,2,1,0:T(2,128)(2,1)}, u32[]{:S(2)}) copy-start(bf16[4,32,2,128]{3,2,1,0:T(2,128)(2,1)} %param.14) | copy-start | bytes 196612
  53.3 2.9 copy-start.1
  58.8 9.0 %all-to-all-start.3 = ((bf16[16,4,2,128]{3,1,2,0:T(4,128)(2,1)}), bf16[16,4,2,128]{3,1,2,0:T(4,128)(2,1)S(1)}, u32[]{:S(2)}, u32[]{:S(2)}) async-start(bf16[16,4,2,128]{3,1,2,0:T(4,128)(2,1)} %copy.133), calls=%async_computation.3 | async-start | bytes 65536 | tf_op jit(solution)/shard_map/all_to_all | solution.py:101
  63.1 17.5 %copy-start.3 = (s32[8]{0:T(128)S(1)}, s32[8]{0:T(128)}, u32[]{:S(2)}) copy-start(s32[8]{0:T(128)} %param.19) | copy-start | bytes 100
  63.2 17.5 %copy-start.4 = (s32[8]{0:T(128)S(1)}, s32[8]{0:T(128)}, u32[]{:S(2)}) copy-start(s32[8]{0:T(128)} %param.17) | copy-start | bytes 100
  67.8 8.3 %all-to-all-start.2 = ((bf16[16,4,512]{2,1,0:T(4,128)(2,1)}), bf16[16,4,512]{2,1,0:T(4,128)(2,1)S(1)}, u32[]{:S(2)}, u32[]{:S(2)}) async-start(bf16[16,4,512]{2,1,0:T(4,128)(2,1)} %reshape.312), calls=%async_computation.2 | async-start | bytes 131072 | tf_op jit(solution)/shard_map/all_to_all | solution.py:100
  76.1 25.4 %all-to-all-start.1 = ((bf16[16,3,2,64,128]{4,3,2,1,0:T(8,128)(2,1)}), bf16[16,3,2,64,128]{4,3,2,1,0:T(8,128)(2,1)}, u32[]{:S(2)}, u32[]{:S(2)}) async-start(bf16[16,3,2,64,128]{4,3,2,1,0:T(8,128)(2,1)} %broadcast_select_fusion), calls=%async_computation.1 | async-start | bytes 3145728 | tf_op jit(solution)/shard_map/all_to_all | solution.py:99
where the time goes:
time: 334 us; the launch traced here: 331 us
  blocking collectives  212 us (63%)
  local copies, waits for them, and re-layouts  38.2 us (11%)
  matrix products  26.1 us (8%)
  waiting for transfers between devices  25.8 us (8%)
  starting transfers between devices  17.2 us (5%)
  other arithmetic  9.98 us (3%)
    psum x1, blocking collectives, local(): summed = lax.psum(partial_sum, 'tp')  212 us
    all_to_all x1, waiting for transfers between devices, local(): lax.all_to_all(slot_pages, 'inst', split_axis=0, concat_axis=0, tiled=True)  19.6 us
    dot_general x1, local copies, waits for them, and re-layouts, local(): jnp.dot(hidden.reshape(-1, width), query_weight, preferred_element_type=j...  11.4 us
    dot_general x1, matrix products, local(): jnp.dot(combined.reshape(-1, combined.shape[-1]), output_weight, preferre...  7.85 us
    dot_general x1, matrix products, local(): jnp.dot(hidden.reshape(-1, width), query_weight, preferred_element_type=j...  6.96 us
  transfers between devices with their start and end apart: 4, of which 3 were waited for; matrix products, arithmetic and copies ran while one was open for 16% of the time, Pallas kernels for 0%

commit v1 on v0

--- a/solution.py
+++ b/solution.py
@@ -64,20 +64,8 @@
 ):
     steps_n, local_rows, width = hidden.shape
     instances = lax.axis_size("inst")
-    query = jnp.dot(hidden.reshape(-1, width), query_weight, preferred_element_type=jnp.float32)
-    query = query.reshape(steps_n, local_rows, GROUP, HD)
-    position = lengths[None, :] + jnp.arange(steps_n, dtype=jnp.int32)[:, None]
-    rotated = rotate(query, position[:, :, None]).astype(jnp.bfloat16)
-    pages = kv_pool[page_table]
-    attended = attend(rotated, pages, lengths, new_kv)
     leaving = mig_req.shape[0]
     order = jnp.arange(leaving, dtype=jnp.int32)
-    hit = mig_req[:, None] == jnp.arange(local_rows, dtype=jnp.int32)[None, :]
-    moved = jnp.min(jnp.where(hit, resume[:, None], steps_n), axis=0)
-    step_ids = jnp.arange(steps_n, dtype=jnp.int32)[:, None]
-    home_rows = jnp.where(
-        (step_ids < moved[None, :])[:, :, None], attended, jnp.zeros_like(attended)
-    )
     dest = mig_dest[:, 0]
     same = dest[None, :] == dest[:, None]
     earlier = order[None, :] < order[:, None]
@@ -88,38 +76,34 @@
     slot_request = jnp.sum(chosen * mig_req[None, :], axis=1)
     filled = jnp.sum(chosen, axis=1)
     slot_resume = jnp.where(filled > 0, jnp.sum(chosen * resume[None, :], axis=1), steps_n)
+    slot_table = jnp.sum(chosen[:, :, None] * page_table[mig_req][None], axis=1)
     slot_pages = jnp.where(
-        (filled > 0)[:, None, None, None, None], pages[slot_request], jnp.zeros_like(pages[:1])
+        (filled > 0)[:, None, None, None, None], kv_pool[slot_table], jnp.zeros((), kv_pool.dtype)
     )
-    slot_query = jnp.transpose(rotated[:, slot_request], (1, 0, 2, 3)).reshape(
-        instances * CAP, steps_n, GROUP * HD
-    )
-    slot_fresh = jnp.transpose(new_kv[:, slot_request], (1, 0, 2, 3))
-    got_pages, got_query, got_fresh = (
-        lax.all_to_all(slot_pages, "inst", split_axis=0, concat_axis=0, tiled=True),
-        lax.all_to_all(slot_query, "inst", split_axis=0, concat_axis=0, tiled=True),
-        lax.all_to_all(slot_fresh, "inst", split_axis=0, concat_axis=0, tiled=True),
-    )
-    slot_meta = jnp.stack([lengths[slot_request], slot_resume], axis=1)
-    got_meta = lax.all_to_all(slot_meta, "inst", split_axis=0, concat_axis=0, tiled=True)
-    arrive_query = jnp.transpose(
-        got_query.reshape(instances * CAP, steps_n, GROUP, HD), (1, 0, 2, 3)
-    )
-    arrive_fresh = jnp.transpose(got_fresh, (1, 0, 2, 3))
-    arrived = attend(arrive_query, got_pages, got_meta[:, 0], arrive_fresh)
-    arrival_rows = jnp.where(
-        (step_ids >= got_meta[None, :, 1])[:, :, None], arrived, jnp.zeros_like(arrived)
-    )
-    combined = jnp.concatenate([home_rows, arrival_rows], axis=1)
+    got_pages = lax.all_to_all(slot_pages, "inst", split_axis=0, concat_axis=0, tiled=True)
+    query = jnp.dot(hidden.reshape(-1, width), query_weight, preferred_element_type=jnp.float32)
+    query = query.reshape(steps_n, local_rows, GROUP, HD)
+    position = lengths[None, :] + jnp.arange(steps_n, dtype=jnp.int32)[:, None]
+    rotated = rotate(query, position[:, :, None]).astype(jnp.bfloat16)
+    pages = kv_pool[page_table]
+    attended = attend(rotated, pages, lengths, new_kv)
+    hit = mig_req[:, None] == jnp.arange(local_rows, dtype=jnp.int32)[None, :]
+    moved = jnp.min(jnp.where(hit, resume[:, None], steps_n), axis=0)
+    step_ids = jnp.arange(steps_n, dtype=jnp.int32)[:, None]
     partial_sum = jnp.dot(
-        combined.reshape(-1, combined.shape[-1]), output_weight, preferred_element_type=jnp.float32
-    )
-    partial_sum = partial_sum.reshape(steps_n, -1, width)
-    summed = lax.psum(partial_sum, "tp")
-    share = width // lax.axis_size("tp")
-    mine = lax.dynamic_slice_in_dim(summed, lax.axis_index("tp") * share, share, 2)
-    mine = mine.astype(jnp.bfloat16)
-    return (mine[:, :local_rows], mine[:, local_rows:], got_pages)
+        attended.reshape(-1, attended.shape[-1]), output_weight, preferred_element_type=jnp.float32
+    ).astype(jnp.bfloat16)
+    tp = lax.axis_size("tp")
+    share = width // tp
+    parts = jnp.transpose(partial_sum.reshape(-1, tp, share), (1, 0, 2))
+    got = lax.all_to_all(parts, "tp", split_axis=0, concat_axis=0, tiled=True)
+    mine = jnp.sum(got.astype(jnp.float32), axis=0).astype(jnp.bfloat16)
+    mine = mine.reshape(steps_n, local_rows, share)
+    zero = jnp.zeros((), jnp.bfloat16)
+    home = jnp.where((step_ids < moved[None, :])[:, :, None], mine, zero)
+    leaver = jnp.where((step_ids >= slot_resume[None, :])[:, :, None], mine[:, slot_request], zero)
+    arrival = lax.all_to_all(leaver, "inst", split_axis=1, concat_axis=1, tiled=True)
+    return (home, arrival, got_pages)
 
 
 def solution(mesh):

time: 334 us -> 136 us (0.41)
  blocking collectives: 212 us -> 0 us
  waiting for transfers between devices: 25.8 us -> 53.6 us
  matrix products: 26.1 us -> 17.7 us
  local copies, waits for them, and re-layouts: 38.2 us -> 33.3 us
  other arithmetic: 9.98 us -> 14.5 us
    psum x1 -> x0, blocking collectives: 212 us -> none  [local(): summed = lax.psum(partial_sum, 'tp')]
    all_to_all x3 -> x2, waiting for transfers between devices: 6.21 us -> 53.6 us  [the longest x1 48.6 us: local(): got = lax.all_to_all(parts, 'tp', split_axis=0, concat_axis=0, tiled=True)]
    all_to_all x1, waiting for transfers between devices: 19.6 us -> 0.01 us  [local(): lax.all_to_all(slot_pages, 'inst', split_axis=0, concat_axis=0, tiled=True)]
    select_n x4 -> x6, other arithmetic: 1.49 us -> 6.23 us  [the longest x1 2.73 us: local(): jnp.where((filled > 0)[:, None, None, None, None], kv_pool[slot_table], j...]
    all_to_all x3 -> x2, starting transfers between devices: 12.7 us -> 9.49 us  [the longest x1 5.61 us: local(): got = lax.all_to_all(parts, 'tp', split_axis=0, concat_axis=0, tiled=True)]
    gather x5 -> x4, local copies, waits for them, and re-layouts: 6.98 us -> 4.39 us  [the longest x1 1.94 us: local(): kv_pool[slot_table]]
  transfers between devices with their start and end apart: 4 -> 3, of which waited for: 3 -> 2; matrix products, arithmetic and copies ran while one was open for 16% -> 33% of each run, Pallas kernels for 0% -> 0%
where the time goes in v1:
time: 136 us; the launch traced here: 135 us
  waiting for transfers between devices  53.6 us (39%)
  local copies, waits for them, and re-layouts  33.3 us (24%)
  matrix products  17.7 us (13%)
  starting transfers between devices  14.8 us (11%)
  other arithmetic  14.5 us (11%)
    all_to_all x1, waiting for transfers between devices, local(): got = lax.all_to_all(parts, 'tp', split_axis=0, concat_axis=0, tiled=True)  48.6 us
    dot_general x1, local copies, waits for them, and re-layouts, local(): jnp.dot(hidden.reshape(-1, width), query_weight, preferred_element_type=j...  11.4 us
    dot_general x1, matrix products, local(): jnp.dot(hidden.reshape(-1, width), query_weight, preferred_element_type=j...  6.96 us
    all_to_all x1, starting transfers between devices, local(): got = lax.all_to_all(parts, 'tp', split_axis=0, concat_axis=0, tiled=True)  5.61 us
    all_to_all x1, starting transfers between devices, local(): lax.all_to_all(slot_pages, 'inst', split_axis=0, concat_axis=0, tiled=True)  5.3 us
    all_to_all x1, waiting for transfers between devices, local(): lax.all_to_all(leaver, 'inst', split_axis=1, concat_axis=1, tiled=True)  5 us
    dot_general x1, matrix products, local(): jnp.dot(attended.reshape(-1, attended.shape[-1]), output_weight, preferre...  4.65 us
    unnamed x17, local copies, waits for them, and re-layouts  4.41 us
  transfers between devices with their start and end apart: 3, of which 2 were waited for; matrix products, arithmetic and copies ran while one was open for 33% of the time, Pallas kernels for 0%

profile of v1, /device:TPU:0, one launch (start us, length us, event | category | flops | bytes accessed | tf_op | source)
XLA Modules:
  0.0 134.7 jit_solution(1806489012281526042)
XLA Ops:
  0.6 0.0 copy-start
  0.6 1.0 convert_reduce_fusion
  1.6 0.7 multiply_add_fusion
  2.3 0.1 fusion.19
  2.4 0.7 compare_select_fusion.2
  3.0 0.8 fusion.21
  3.8 0.8 copy.138
  4.6 0.6 gather_fusion.2
  5.1 0.1 copy.139
  5.2 0.1 multiply_reduce_fusion
  5.3 0.1 copy.140
  5.4 0.1 reshape.253
  5.5 0.0 copy-done
  5.5 1.9 %gather_fusion.3 = bf16[48,2,64,128]{3,2,1,0:T(8,128)(2,1)} fusion(bf16[96,2,64,128]{3,2,1,0:T(8,128)(2,1)S(1)} %copy-done, s32[1024]{0:T(1024)S(1)} %pad_clamp_fusion), kind=kCustom, calls=%fused_computation.3 | custom fusion | bytes 3145920 | tf_op jit(solution)/shard_map/gather | solution.py:81
  7.5 2.7 %broadcast_select_fusion = bf16[16,3,2,64,128]{4,3,2,1,0:T(8,128)(2,1)} fusion(bf16[16,3,2,64,128]{4,3,2,1,0:T(8,128)(2,1)} %bitcast.81, pred[16]{0:T(512)(128)(4,1)S(1)} %broadcast_compare_fusion), kind=kLoop, calls=%fused_computation.8 | loop fusion | flops 786432 | bytes 3145744 | tf_op jit(solution)/shard_map/jit(_where)/select_n | solution.py:80
  10.2 5.3 %all-to-all-start.2 = ((bf16[16,3,2,64,128]{4,3,2,1,0:T(8,128)(2,1)}), bf16[16,3,2,64,128]{4,3,2,1,0:T(8,128)(2,1)}, u32[]{:S(2)}, u32[]{:S(2)}) async-start(bf16[16,3,2,64,128]{4,3,2,1,0:T(8,128)(2,1)} %broadcast_select_fusion), calls=%async_computation.2 | async-start | bytes 3145728 | tf_op jit(solution)/shard_map/all_to_all | solution.py:83
  15.5 0.0 copy-done.3
  15.5 0.0 copy-done.4
  15.6 0.1 iota_compare_fusion
  15.6 11.4 %copy.147 = bf16[512,8192]{1,0:T(8,128)(2,1)} copy(bf16[512,8192]{0,1:T(8,128)(2,1)} %bitcast.76) | data formatting | bytes 16777216 | tf_op jit(solution)/shard_map/dot_general | solution.py:84
  27.1 7.0 %fusion = f32[4,32,4,128]{3,1,2,0:T(8,128)S(1)} fusion(bf16[4,128,8192,1]{2,1,0,3:T(8,128)(2,1)} %bitcast.77, bf16[4,32,8192]{2,1,0:T(8,128)(2,1)} %param.10), kind=kOutput, calls=%fused_computation.6 | convolution fusion | flops 1073741824 | bytes 10747904 | tf_op jit(solution)/shard_map/dot_general | solution.py:84
  34.0 0.1 slice_negate_fusion
  34.2 0.1 broadcast_multiply_fusion
  34.3 0.3 fusion.16
  34.6 0.0 copy-done.1
  34.6 0.7 fusion.24
  35.3 0.1 fusion.7
  35.5 2.0 %fusion.12 = f32[32,4,4,4]{2,3,1,0:T(4,128)} fusion(bf16[4,32,4,128]{3,1,2,0:T(8,128)(2,1)S(1)} %fusion.7, bf16[4,32,1,128]{3,2,1,0:T(2,128)(2,1)S(1)} %get-tuple-element.32), kind=kOutput, calls=%fused_computation.28 | convolution fusion | flops 524288 | bytes 172032 | tf_op jit(solution)/shard_map/sbgd,ubd->bsgu/dot_general | solution.py:32
  37.4 1.1 copy.128
  38.6 0.1 fusion.17
  38.7 0.1 copy.129
  38.8 0.1 copy.121
  38.9 0.1 reshape.229
  39.0 2.7 %gather_fusion = bf16[96,2,64,128]{3,2,1,0:T(8,128)(2,1)} fusion(bf16[96,2,64,128]{3,2,1,0:T(8,128)(2,1)S(1)} %copy-done, s32[1024]{0:T(1024)S(1)} %pad_clamp_fusion.3), kind=kCustom, calls=%fused_computation | custom fusion | bytes 6291840 | tf_op jit(solution)/shard_map/gather | solution.py:88
  41.7 3.7 %fusion.23 = (bf16[32,3,1,64,128]{4,3,2,1,0:T(8,128)(2,1)S(1)}, bf16[32,3,1,64,128]{4,3,2,1,0:T(8,128)(2,1)}) fusion(bf16[32,3,2,64,128]{4,3,2,1,0:T(8,128)(2,1)} %bitcast.75), kind=kLoop, calls=%fused_computation.71 | loop fusion | bytes 6291456 | tf_op jit(solution)/shard_map/slice | solution.py:27
  45.4 1.8 %fusion.25 = (f32[32,4,4]{2,1,0:T(4,128)S(1)}, f32[32,4,4,192]{3,2,1,0:T(4,128)}) fusion(bf16[32,192,128,1]{2,1,3,0:T(8,128)(2,1)S(1)} %bitcast.80, bf16[4,32,4,128]{3,1,2,0:T(8,128)(2,1)S(1)} %fusion.7, pred[32,192]{1,0:T(8,128)(4,1)S(1)} %iota_compare_fusion), kind=kOutput, calls=%fused_computation.73 | convolution fusion | flops 25460224 | bytes 2105344 | tf_op jit(solution)/shard_map/sbgd,bld->bsgl/dot_general | solution.py:30
  47.2 0.1 copy.130
  47.3 1.5 %fusion.5 = f32[32,4,4]{2,1,0:T(4,128)S(1)} fusion(f32[32,4,4,192]{3,2,1,0:T(4,128)} %get-tuple-element.36, f32[32,4,4]{2,1,0:T(4,128)S(1)} %max.7), kind=kLoop, calls=%fused_computation.18 | loop fusion | flops 196096 | bytes 397312 | tf_op jit(solution)/shard_map/reduce_sum | solution.py:43
  48.8 0.1 fusion.18
  48.9 0.1 copy.131
  49.1 0.1 copy.132
  49.2 0.1 divide_convert_fusion.2
  49.3 0.2 copy.134
  49.5 0.0 copy-start.2
  49.5 2.1 %convolution_bitcast_fusion.1 = f32[4,32,4,128]{3,2,0,1:T(4,128)S(1)} fusion(bf16[32,192,128,1]{2,1,3,0:T(8,128)(2,1)} %bitcast.84, f32[32,4,4,192]{3,2,1,0:T(4,128)} %get-tuple-element.36, f32[32,4,4]{2,1,0:T(4,128)S(1)} %add.73, f32[32,4,4]{2,1,0:T(4,128)S(1)} %max.7), kind=kOutput, calls=%fused_computation.13 | convolution fusion | flops 25460736 | bytes 2232320 | tf_op jit(solution)/shard_map/bsgl,bld->sbgd/dot_general | solution.py:46
  51.6 0.0 copy-done.2
  51.6 0.2 fusion.4
  51.9 4.6 %convolution_convert_fusion = bf16[128,8192]{1,0:T(8,128)(2,1)S(1)} fusion(bf16[512,8192]{1,0:T(8,128)(2,1)} %param.12, bf16[16,8,4,128]{3,2,1,0:T(4,128)(2,1)S(1)} %bitcast.85), kind=kOutput, calls=%fused_computation.4 | convolution fusion | flops 1074790400 | bytes 10616832 | tf_op jit(solution)/shard_map/dot_general | solution.py:93
  56.5 1.5 %copy.169 = bf16[16,4,8,2048]{3,2,0,1:T(8,128)(2,1)} copy(bf16[16,4,8,2048]{3,2,1,0:T(8,128)(2,1)S(1)} %bitcast.79) | data formatting | bytes 4194304 | tf_op jit(solution)/shard_map/reshape | solution.py:98
  58.0 0.0 all-to-all-done.2
  58.0 5.6 %all-to-all-start = ((bf16[4,128,2048]{2,1,0:T(8,128)(2,1)}), bf16[4,128,2048]{2,1,0:T(8,128)(2,1)}, u32[]{:S(2)}, u32[]{:S(2)}) async-start(bf16[4,128,2048]{2,1,0:T(8,128)(2,1)} %bitcast.78), calls=%async_computation | async-start | bytes 4194304 | tf_op jit(solution)/shard_map/all_to_all | solution.py:99
  63.7 0.0 copy-done.6
  63.7 0.1 select_reduce_fusion.2
  63.8 0.1 iota_compare_fusion.1
  63.8 48.6 %all-to-all-done = bf16[4,128,2048]{2,1,0:T(8,128)(2,1)} async-done(((bf16[4,128,2048]{2,1,0:T(8,128)(2,1)}), bf16[4,128,2048]{2,1,0:T(8,128)(2,1)}, u32[]{:S(2)}, u32[]{:S(2)}) %all-to-all-start) | async-done | bytes 2097184 | tf_op jit(solution)/shard_map/all_to_all | solution.py:99
  112.5 2.9 %reduce_sum.81 = bf16[128,2048]{1,0:T(8,128)(2,1)} reduce(bf16[4,128,2048]{2,1,0:T(8,128)(2,1)} %all-to-all-done, bf16[]{:T(256)} %constant.7.clone.1), dimensions={0}, to_apply=%region_5.6 | reduce | flops 786432 | bytes 2621442 | tf_op jit(solution)/shard_map/reduce_sum | solution.py:100
  115.4 2.2 %copy.137 = bf16[4,32,2048]{2,0,1:T(4,128)(2,1)} copy(bf16[4,32,2048]{2,1,0:T(8,128)(2,1)} %bitcast.82) | data formatting | bytes 1048576 | tf_op jit(solution)/shard_map/reshape | solution.py:101
  117.6 1.8 %gather_fusion.1 = bf16[16,4,2048]{2,1,0:T(4,128)(2,1)S(1)} fusion(bf16[4,32,2048]{2,0,1:T(4,128)(2,1)} %copy.137, s32[1024]{0:T(1024)S(1)} %pad_clamp_fusion.2), kind=kCustom, calls=%fused_computation.1 | custom fusion | bytes 524352 | tf_op jit(solution)/shard_map/gather | solution.py:104
  119.4 0.9 bitcast_select_fusion
  120.3 3.9 %all-to-all-start.1 = ((bf16[4,16,2048]{2,0,1:T(4,128)(2,1)}), bf16[4,16,2048]{2,0,1:T(4,128)(2,1)S(1)}, u32[]{:S(2)}, u32[]{:S(2)}) async-start(bf16[4,16,2048]{2,0,1:T(4,128)(2,1)} %bitcast_select_fusion), calls=%async_computation.1 | async-start | bytes 524288 | tf_op jit(solution)/shard_map/all_to_all | solution.py:105
  124.2 1.9 %broadcast_select_fusion.1 = bf16[4,32,2048]{2,1,0:T(8,128)(2,1)} fusion(bf16[4,32,2048]{2,1,0:T(8,128)(2,1)} %bitcast.83, pred[4,32]{1,0:T(4,128)(4,1)S(1)} %iota_compare_fusion.6), kind=kLoop, calls=%fused_computation.17 | loop fusion | flops 262144 | bytes 1048704 | tf_op jit(solution)/shard_map/jit(_where)/select_n | solution.py:103
  126.1 5.0 %all-to-all-done.1 = bf16[4,16,2048]{2,0,1:T(4,128)(2,1)S(1)} async-done(((bf16[4,16,2048]{2,0,1:T(4,128)(2,1)}), bf16[4,16,2048]{2,0,1:T(4,128)(2,1)S(1)}, u32[]{:S(2)}, u32[]{:S(2)}) %all-to-all-start.1) | async-done | bytes 262176 | tf_op jit(solution)/shard_map/all_to_all | solution.py:105
  131.1 0.9 copy.141
  132.0 2.8 %copy.171 = bf16[16,3,2,64,128]{4,3,2,1,0:T(8,128)(2,1)} copy(bf16[16,3,2,64,128]{4,3,2,1,0:T(8,128)(2,1)} %all-to-all-done.2) | data formatting | bytes 3145728
  (22 shorter events, 0.2 us)
Async XLA Ops:
  0.6 4.9 %copy-start = (bf16[96,2,64,128]{3,2,1,0:T(8,128)(2,1)S(1)}, bf16[96,2,64,128]{3,2,1,0:T(8,128)(2,1)}, u32[]{:S(2)}) copy-start(bf16[96,2,64,128]{3,2,1,0:T(8,128)(2,1)} %param.13) | copy-start | bytes 9437188
  10.2 5.3 %copy-start.3 = (s32[32,3]{0,1:T(4,128)S(1)}, s32[32,3]{0,1:T(4,128)}, u32[]{:S(2)}) copy-start(s32[32,3]{0,1:T(4,128)} %param.16) | copy-start | bytes 1156
  10.2 5.4 %copy-start.4 = (s32[32]{0:T(128)S(1)}, s32[32]{0:T(128)}, u32[]{:S(2)}) copy-start(s32[32]{0:T(128)} %param.15) | copy-start | bytes 388
  10.2 47.8 %all-to-all-start.2 = ((bf16[16,3,2,64,128]{4,3,2,1,0:T(8,128)(2,1)}), bf16[16,3,2,64,128]{4,3,2,1,0:T(8,128)(2,1)}, u32[]{:S(2)}, u32[]{:S(2)}) async-start(bf16[16,3,2,64,128]{4,3,2,1,0:T(8,128)(2,1)} %broadcast_select_fusion), calls=%async_computation.2 | async-start | bytes 3145728 | tf_op jit(solution)/shard_map/all_to_all | solution.py:83
  27.1 7.5 %copy-start.1 = (bf16[4,32,2,128]{3,2,1,0:T(2,128)(2,1)S(1)}, bf16[4,32,2,128]{3,2,1,0:T(2,128)(2,1)}, u32[]{:S(2)}) copy-start(bf16[4,32,2,128]{3,2,1,0:T(2,128)(2,1)} %param.14) | copy-start | bytes 196612
  49.5 2.1 %copy-start.2 = (bf16[4,32,1,128]{3,2,1,0:T(2,128)(2,1)S(1)}, bf16[4,32,1,128]{3,2,1,0:T(2,128)(2,1)}, u32[]{:S(2)}) copy-start(bf16[4,32,1,128]{3,2,1,0:T(2,128)(2,1)} %get-tuple-element.31) | copy-start | bytes 98308
  58.0 5.6 %copy-start.5 = (s32[8]{0:T(128)S(1)}, s32[8]{0:T(128)}, u32[]{:S(2)}) copy-start(s32[8]{0:T(128)} %param.19) | copy-start | bytes 100
  58.0 5.6 %copy-start.6 = (s32[8]{0:T(128)S(1)}, s32[8]{0:T(128)}, u32[]{:S(2)}) copy-start(s32[8]{0:T(128)} %param.17) | copy-start | bytes 100
  58.0 54.4 %all-to-all-start = ((bf16[4,128,2048]{2,1,0:T(8,128)(2,1)}), bf16[4,128,2048]{2,1,0:T(8,128)(2,1)}, u32[]{:S(2)}, u32[]{:S(2)}) async-start(bf16[4,128,2048]{2,1,0:T(8,128)(2,1)} %bitcast.78), calls=%async_computation | async-start | bytes 4194304 | tf_op jit(solution)/shard_map/all_to_all | solution.py:99
  120.3 10.8 %all-to-all-start.1 = ((bf16[4,16,2048]{2,0,1:T(4,128)(2,1)}), bf16[4,16,2048]{2,0,1:T(4,128)(2,1)S(1)}, u32[]{:S(2)}, u32[]{:S(2)}) async-start(bf16[4,16,2048]{2,0,1:T(4,128)(2,1)} %bitcast_select_fusion), calls=%async_computation.1 | async-start | bytes 524288 | tf_op jit(solution)/shard_map/all_to_all | solution.py:105

commit v2 on v1

--- a/solution.py
+++ b/solution.py
@@ -1,6 +1,10 @@
+import functools
+
 import jax
 import jax.numpy as jnp
 from jax import lax
+from jax.experimental import pallas as pl
+from jax.experimental.pallas import tpu as pltpu
 from jax.sharding import PartitionSpec as P
 
 HD = 128
@@ -48,6 +52,232 @@
         "bsgu,ubd->sbgd", newer_p, fresh[:, :, 1], preferred_element_type=jnp.float32
     )
     return result.astype(jnp.bfloat16).reshape(steps_n, count, -1)
+
+
+MESH = pl.DeviceIdType.MESH
+
+
+def project_kernel(
+    n, ni, chunks, att_ref, w_ref, keep_ref, sel_ref, pages_ref,
+    home_ref, arrive_ref, got_ref,
+    w_buf, part, up_in, down_in, up_out, down_out, leave,
+    w_sem, up_send, up_recv, down_send, down_recv, page_send, page_recv, row_send, row_recv, own_sem,
+):
+    z = lax.axis_index("tp")
+    me = lax.axis_index("inst")
+    width = part.shape[2]
+    low = z < n // 2
+
+    def block_of(k):
+        return jnp.where(low, n - 1 - k // chunks, k // chunks)
+
+    def w_copy(k):
+        column = (block_of(k) * chunks + k % chunks) * width
+        return pltpu.make_async_copy(
+            w_ref.at[:, pl.ds(pl.multiple_of(column, width), width)], w_buf.at[k], w_sem.at[k]
+        )
+
+    for k in range(n * chunks):
+        w_copy(k).start()
+
+    barrier = pltpu.get_barrier_semaphore()
+    for k in range(1, ni):
+        pl.semaphore_signal(
+            barrier, inc=1, device_id={"inst": lax.rem(me + k, ni)}, device_id_type=MESH
+        )
+
+    @pl.when(z > 0)
+    def _():
+        pl.semaphore_signal(barrier, inc=1, device_id={"tp": z - 1}, device_id_type=MESH)
+
+    @pl.when(z < n - 1)
+    def _():
+        pl.semaphore_signal(barrier, inc=1, device_id={"tp": z + 1}, device_id_type=MESH)
+
+    pl.semaphore_wait(barrier, ni - 1 + (z > 0).astype(jnp.int32) + (z < n - 1).astype(jnp.int32))
+
+    cap = pages_ref.shape[0] // ni
+
+    def page_copy(k):
+        to = lax.rem(me + k, ni)
+        return pltpu.make_async_remote_copy(
+            src_ref=pages_ref.at[pl.ds(to * cap, cap)],
+            dst_ref=got_ref.at[pl.ds(me * cap, cap)],
+            send_sem=page_send.at[k],
+            recv_sem=page_recv.at[k],
+            device_id={"inst": to},
+            device_id_type=MESH,
+        )
+
+    own_pages = pltpu.make_async_copy(
+        pages_ref.at[pl.ds(me * cap, cap)], got_ref.at[pl.ds(me * cap, cap)], own_sem.at[0]
+    )
+
+    def up_copy(j):
+        return pltpu.make_async_remote_copy(
+            src_ref=up_out.at[j], dst_ref=up_in.at[j],
+            send_sem=up_send.at[j], recv_sem=up_recv.at[j],
+            device_id={"tp": jnp.minimum(z + 1, n - 1)}, device_id_type=MESH,
+        )
+
+    def down_copy(j):
+        return pltpu.make_async_remote_copy(
+            src_ref=down_out.at[j], dst_ref=down_in.at[j],
+            send_sem=down_send.at[j], recv_sem=down_recv.at[j],
+            device_id={"tp": jnp.maximum(z - 1, 0)}, device_id_type=MESH,
+        )
+
+    def compute(k, carry):
+        w_copy(k).wait()
+        value = jnp.dot(att_ref[...], w_buf[k], preferred_element_type=jnp.float32)
+        part[block_of(k) * chunks + k % chunks] = value
+
+        @pl.when((z == 0) & (k < (n - 1) * chunks))
+        def _():
+            up_out[k] = value.astype(jnp.bfloat16)
+            up_copy(k).start()
+
+        @pl.when((z == n - 1) & (k < (n - 1) * chunks))
+        def _():
+            down_out[k] = value.astype(jnp.bfloat16)
+            down_copy(k).start()
+
+        return carry
+
+    lax.fori_loop(0, n * chunks, compute, 0)
+    for k in range(1, ni):
+        page_copy(k).start()
+    own_pages.start()
+
+    up_lag = jnp.maximum(z - 1, 0)
+    down_lag = jnp.maximum(n - 2 - z, 0)
+
+    def relay(j, carry):
+        ju = j - up_lag
+        jd = j - down_lag
+
+        @pl.when((z > 0) & (ju >= 0) & (ju < (n - z) * chunks))
+        def _():
+            up_copy(ju).wait_recv()
+            spot = (n - 1 - ju // chunks) * chunks + ju % chunks
+            value = part[spot] + up_in[ju].astype(jnp.float32)
+
+            @pl.when(ju < (n - 1 - z) * chunks)
+            def _():
+                up_out[ju] = value.astype(jnp.bfloat16)
+                up_copy(ju).start()
+
+            @pl.when(ju >= (n - 1 - z) * chunks)
+            def _():
+                part[spot] = value
+
+        @pl.when((z < n - 1) & (jd >= 0) & (jd < (z + 1) * chunks))
+        def _():
+            down_copy(jd).wait_recv()
+            value = part[jd] + down_in[jd].astype(jnp.float32)
+
+            @pl.when(jd < z * chunks)
+            def _():
+                down_out[jd] = value.astype(jnp.bfloat16)
+                down_copy(jd).start()
+
+            @pl.when(jd >= z * chunks)
+            def _():
+                part[jd] = value
+
+        return carry
+
+    lax.fori_loop(0, (n - 1) * chunks + n - 2, relay, 0)
+
+    half = chunks // 2
+    for c in range(half):
+        pieces = []
+        for d in (c, c + half):
+            mine = part[z * chunks + d].astype(jnp.bfloat16)
+            home_ref[:, d * width:(d + 1) * width] = jnp.where(
+                keep_ref[...] > 0, mine, jnp.zeros_like(mine)
+            )
+            rows = jnp.dot(sel_ref[...], mine, preferred_element_type=jnp.float32)
+            pieces.append(rows.reshape(ni, -1, width))
+        leave[:, :, c * width:(c + 1) * width] = jnp.concatenate(pieces, axis=1).astype(jnp.bfloat16)
+
+    def row_copy(k):
+        to = lax.rem(me + k, ni)
+        return pltpu.make_async_remote_copy(
+            src_ref=leave.at[to],
+            dst_ref=arrive_ref.at[me],
+            send_sem=row_send.at[k],
+            recv_sem=row_recv.at[k],
+            device_id={"inst": to},
+            device_id_type=MESH,
+        )
+
+    own_rows = pltpu.make_async_copy(leave.at[me], arrive_ref.at[me], own_sem.at[1])
+    for k in range(1, ni):
+        row_copy(k).start()
+    own_rows.start()
+
+    def drain(j, carry):
+        @pl.when((z < n - 1) & (j < (n - 1 - z) * chunks))
+        def _():
+            up_copy(j).wait_send()
+
+        @pl.when((z > 0) & (j < z * chunks))
+        def _():
+            down_copy(j).wait_send()
+
+        return carry
+
+    lax.fori_loop(0, (n - 1) * chunks, drain, 0)
+    for k in range(1, ni):
+        page_copy(k).wait()
+    own_pages.wait()
+    for k in range(1, ni):
+        row_copy(k).wait()
+    own_rows.wait()
+
+
+def project(attended, output_weight, keep, select, pages):
+    n = lax.axis_size("tp")
+    ni = lax.axis_size("inst")
+    rows, inner = attended.shape
+    width = output_weight.shape[1]
+    share = width // n
+    chunk = min(512, share // 2)
+    chunks = share // chunk
+    hops = (n - 1) * chunks
+    slot_rows = select.shape[0] // ni
+    vmem = pl.BlockSpec(memory_space=pltpu.VMEM)
+    hbm = pl.BlockSpec(memory_space=pl.ANY)
+    relay = pltpu.VMEM((hops, rows, chunk), jnp.bfloat16)
+    dma = pltpu.SemaphoreType.DMA
+    return pl.pallas_call(
+        functools.partial(project_kernel, n, ni, chunks),
+        out_shape=(
+            jax.ShapeDtypeStruct((rows, share), jnp.bfloat16),
+            jax.ShapeDtypeStruct((ni, 2 * slot_rows, share // 2), jnp.bfloat16),
+            jax.ShapeDtypeStruct(pages.shape, pages.dtype),
+        ),
+        in_specs=[vmem, hbm, vmem, vmem, hbm],
+        out_specs=(vmem, hbm, hbm),
+        scratch_shapes=[
+            pltpu.VMEM((n * chunks, inner, chunk), jnp.bfloat16),
+            pltpu.VMEM((n * chunks, rows, chunk), jnp.float32),
+            relay, relay, relay, relay,
+            pltpu.VMEM((ni, 2 * slot_rows, share // 2), jnp.bfloat16),
+            dma((n * chunks,)),
+            dma((hops,)), dma((hops,)), dma((hops,)), dma((hops,)),
+            dma((ni,)), dma((ni,)), dma((ni,)), dma((ni,)), dma((2,)),
+        ],
+        compiler_params=pltpu.CompilerParams(
+            collective_id=0, has_side_effects=True, vmem_limit_bytes=40 * 1024 * 1024
+        ),
+        cost_estimate=pl.CostEstimate(
+            flops=2 * rows * inner * width,
+            bytes_accessed=2 * inner * width + 4 * pages.size,
+            transcendentals=0,
+        ),
+    )(attended, output_weight, keep, select, pages)
 
 
 def local(
@@ -80,7 +310,6 @@
     slot_pages = jnp.where(
         (filled > 0)[:, None, None, None, None], kv_pool[slot_table], jnp.zeros((), kv_pool.dtype)
     )
-    got_pages = lax.all_to_all(slot_pages, "inst", split_axis=0, concat_axis=0, tiled=True)
     query = jnp.dot(hidden.reshape(-1, width), query_weight, preferred_element_type=jnp.float32)
     query = query.reshape(steps_n, local_rows, GROUP, HD)
     position = lengths[None, :] + jnp.arange(steps_n, dtype=jnp.int32)[:, None]
@@ -90,19 +319,19 @@
     hit = mig_req[:, None] == jnp.arange(local_rows, dtype=jnp.int32)[None, :]
     moved = jnp.min(jnp.where(hit, resume[:, None], steps_n), axis=0)
     step_ids = jnp.arange(steps_n, dtype=jnp.int32)[:, None]
-    partial_sum = jnp.dot(
-        attended.reshape(-1, attended.shape[-1]), output_weight, preferred_element_type=jnp.float32
-    ).astype(jnp.bfloat16)
-    tp = lax.axis_size("tp")
-    share = width // tp
-    parts = jnp.transpose(partial_sum.reshape(-1, tp, share), (1, 0, 2))
-    got = lax.all_to_all(parts, "tp", split_axis=0, concat_axis=0, tiled=True)
-    mine = jnp.sum(got.astype(jnp.float32), axis=0).astype(jnp.bfloat16)
-    mine = mine.reshape(steps_n, local_rows, share)
-    zero = jnp.zeros((), jnp.bfloat16)
-    home = jnp.where((step_ids < moved[None, :])[:, :, None], mine, zero)
-    leaver = jnp.where((step_ids >= slot_resume[None, :])[:, :, None], mine[:, slot_request], zero)
-    arrival = lax.all_to_all(leaver, "inst", split_axis=1, concat_axis=1, tiled=True)
+    keep = (step_ids < moved[None, :]).astype(jnp.int32).reshape(-1, 1)
+    goes = step_ids[None] >= slot_resume[:, None, None]
+    row_ids = jnp.arange(local_rows, dtype=jnp.int32)
+    picked = (slot_request[:, None] == row_ids[None, :]) & (filled > 0)[:, None]
+    same_step = step_ids == jnp.arange(steps_n, dtype=jnp.int32)[None, :]
+    select = (goes & same_step[None])[:, :, :, None] & picked[:, None, None, :]
+    select = select.astype(jnp.bfloat16).reshape(instances * CAP * steps_n, steps_n * local_rows)
+    home, arrive, got_pages = project(
+        attended.reshape(-1, attended.shape[-1]), output_weight, keep, select, slot_pages
+    )
+    home = home.reshape(steps_n, local_rows, -1)
+    arrive = arrive.reshape(instances, 2, CAP, steps_n, -1)
+    arrival = jnp.transpose(arrive, (3, 0, 2, 1, 4)).reshape(steps_n, instances * CAP, -1)
     return (home, arrival, got_pages)
 
 

time: 136 us -> 105 us (0.77)
  the two profiles are of different devices: /device:TPU:0 before, /device:TPU:17 now
where the time goes in v2:
time: 105 us
  Pallas kernels  45.3 us (43%)
  local copies, waits for them, and re-layouts  39.2 us (37%)
  matrix products  13 us (12%)
  other arithmetic  6.26 us (6%)
    pallas_call x1, Pallas kernels, project(): pl.pallas_call(functools.partial(project_kernel, n, ni, chunks), out_shap...  45.3 us
    unnamed x28, local copies, waits for them, and re-layouts  12.3 us
    dot_general x1, local copies, waits for them, and re-layouts, local(): jnp.dot(hidden.reshape(-1, width), query_weight, preferred_element_type=j...  11.6 us
    dot_general x1, matrix products, local(): jnp.dot(hidden.reshape(-1, width), query_weight, preferred_element_type=j...  6.95 us
    slice x1, local copies, waits for them, and re-layouts, attend(): keys = pages[:, :, 0].reshape(count, -1, depth)  3.73 us
    select_n x1, other arithmetic, local(): jnp.where((filled > 0)[:, None, None, None, None], kv_pool[slot_table], j...  2.72 us
    gather x1, local copies, waits for them, and re-layouts, local(): pages = kv_pool[page_table]  2.72 us

profile of v2, /device:TPU:17, one launch (start us, length us, event | category | flops | bytes accessed | tf_op | source)
XLA Modules:
  0.0 104.8 jit_solution(8084403209561953887)
XLA Ops:
  0.6 0.0 copy-start
  0.6 11.6 %copy.117 = bf16[512,8192]{1,0:T(8,128)(2,1)} copy(bf16[512,8192]{0,1:T(8,128)(2,1)} %bitcast.65) | data formatting | bytes 16777216 | tf_op jit(solution)/shard_map/dot_general | solution.py:313
  12.2 7.0 %fusion = f32[4,32,4,128]{3,1,2,0:T(8,128)S(1)} fusion(bf16[4,128,8192,1]{2,1,0,3:T(8,128)(2,1)} %bitcast.66, bf16[4,32,8192]{2,1,0:T(8,128)(2,1)} %param.10), kind=kOutput, calls=%fused_computation.3 | convolution fusion | flops 1073741824 | bytes 10747904 | tf_op jit(solution)/shard_map/dot_general | solution.py:313
  19.2 0.0 copy-start.6
  19.2 0.0 copy-start.7
  19.2 0.1 slice_negate_fusion
  19.4 0.1 broadcast_multiply_fusion
  19.5 0.3 fusion.14
  19.8 0.1 fusion.7
  19.9 0.1 copy-done.6
  20.0 0.1 fusion.23
  20.1 2.0 %fusion.10 = f32[32,4,4,4]{2,3,1,0:T(4,128)} fusion(bf16[4,32,4,128]{3,1,2,0:T(8,128)(2,1)S(1)} %fusion.7, bf16[4,32,1,128]{3,2,1,0:T(2,128)(2,1)S(1)} %get-tuple-element.17), kind=kOutput, calls=%fused_computation.23 | convolution fusion | flops 524288 | bytes 172032 | tf_op jit(solution)/shard_map/sbgd,ubd->bsgu/dot_general | solution.py:36
  22.1 1.1 %copy.99 = f32[32,4,4,4]{0,3,2,1:T(4,128)S(1)} copy(f32[32,4,4,4]{2,3,1,0:T(4,128)} %fusion.10) | data formatting | bytes 16384 | tf_op jit(solution)/shard_map/sbgd,ubd->bsgu/dot_general | solution.py:36
  23.2 0.1 fusion.15
  23.3 0.1 copy.100
  23.5 0.0 copy-done.7
  23.5 0.1 copy.92
  23.6 0.1 reshape.289
  23.7 2.7 %gather_fusion = bf16[96,2,64,128]{3,2,1,0:T(8,128)(2,1)} fusion(bf16[96,2,64,128]{3,2,1,0:T(8,128)(2,1)S(1)} %copy-done, s32[1024]{0:T(1024)S(1)} %pad_clamp_fusion.2), kind=kCustom, calls=%fused_computation | custom fusion | bytes 6291840 | tf_op jit(solution)/shard_map/gather | solution.py:317
  26.4 3.7 %fusion.22 = (bf16[32,3,1,64,128]{4,3,2,1,0:T(8,128)(2,1)S(1)}, bf16[32,3,1,64,128]{4,3,2,1,0:T(8,128)(2,1)}) fusion(bf16[32,3,2,64,128]{4,3,2,1,0:T(8,128)(2,1)} %bitcast.64), kind=kLoop, calls=%fused_computation.68 | loop fusion | bytes 6291456 | tf_op jit(solution)/shard_map/slice | solution.py:31
  30.1 0.1 iota_compare_fusion
  30.2 1.8 %fusion.24 = (f32[32,4,4]{2,1,0:T(4,128)S(1)}, f32[32,4,4,192]{3,2,1,0:T(4,128)}) fusion(bf16[32,192,128,1]{2,1,3,0:T(8,128)(2,1)S(1)} %bitcast.67, bf16[4,32,4,128]{3,1,2,0:T(8,128)(2,1)S(1)} %fusion.7, pred[32,192]{1,0:T(8,128)(4,1)S(1)} %iota_compare_fusion), kind=kOutput, calls=%fused_computation.70 | convolution fusion | flops 25460224 | bytes 2105344 | tf_op jit(solution)/shard_map/sbgd,bld->bsgl/dot_general | solution.py:34
  32.0 0.1 copy.101
  32.1 0.1 fusion.16
  32.2 0.1 copy.102
  32.4 1.4 %fusion.5 = f32[32,4,4]{2,1,0:T(4,128)S(1)} fusion(f32[32,4,4,192]{3,2,1,0:T(4,128)} %get-tuple-element.21, f32[32,4,4]{2,1,0:T(4,128)S(1)} %max.7), kind=kLoop, calls=%fused_computation.14 | loop fusion | flops 196096 | bytes 397312 | tf_op jit(solution)/shard_map/reduce_sum | solution.py:47
  33.8 0.1 copy.103
  33.9 0.1 divide_convert_fusion.2
  34.0 0.2 copy.105
  34.3 0.0 copy-start.11
  34.3 0.0 copy-start.9
  34.3 0.0 copy-start.10
  34.3 2.1 %convolution_bitcast_fusion.1 = f32[4,32,4,128]{3,2,0,1:T(4,128)S(1)} fusion(bf16[32,192,128,1]{2,1,3,0:T(8,128)(2,1)} %bitcast.69, f32[32,4,4,192]{3,2,1,0:T(4,128)} %get-tuple-element.21, f32[32,4,4]{2,1,0:T(4,128)S(1)} %add.68, f32[32,4,4]{2,1,0:T(4,128)S(1)} %max.7), kind=kOutput, calls=%fused_computation.10 | convolution fusion | flops 25460736 | bytes 2232320 | tf_op jit(solution)/shard_map/bsgl,bld->sbgd/dot_general | solution.py:50
  36.4 0.2 fusion.4
  36.7 0.2 convert_reduce_fusion
  36.9 0.1 select_reduce_fusion.1
  37.0 0.1 fusion.17
  37.1 0.1 iota_compare_fusion.2
  37.2 0.1 broadcast_and_fusion
  37.3 0.1 and_convert_fusion
  37.4 0.1 reshape.286.sel_ref
  37.5 0.1 fusion.18
  37.6 0.1 copy.107
  37.7 0.6 gather_fusion.1
  38.2 0.1 copy.108
  38.3 0.1 multiply_reduce_fusion
  38.4 0.1 copy.109
  38.5 0.1 reshape.305
  38.6 1.9 %gather_fusion.2 = bf16[48,2,64,128]{3,2,1,0:T(8,128)(2,1)} fusion(bf16[96,2,64,128]{3,2,1,0:T(8,128)(2,1)S(1)} %copy-done, s32[1024]{0:T(1024)S(1)} %pad_clamp_fusion), kind=kCustom, calls=%fused_computation.2 | custom fusion | bytes 3145920 | tf_op jit(solution)/shard_map/gather | solution.py:311
  40.5 2.7 %broadcast_select_fusion.pages_ref = bf16[16,3,2,64,128]{4,3,2,1,0:T(8,128)(2,1)} fusion(bf16[16,3,2,64,128]{4,3,2,1,0:T(8,128)(2,1)} %bitcast.68, pred[16]{0:T(512)(128)(4,1)S(1)} %broadcast_compare_fusion), kind=kLoop, calls=%fused_computation.5 | loop fusion | flops 786432 | bytes 3145744 | tf_op jit(solution)/shard_map/jit(_where)/select_n | solution.py:310
  43.3 0.1 select_reduce_fusion.2
  43.4 0.1 reshape.321.keep_ref
  43.5 0.0 copy-start.1
  43.5 3.4 %copy-done.1 = bf16[512,8192]{1,0:T(8,128)(2,1)S(1)} copy-done((bf16[512,8192]{1,0:T(8,128)(2,1)S(1)}, bf16[512,8192]{1,0:T(8,128)(2,1)}, u32[]{:S(2)}) %copy-start.1) | copy-done | bytes 8388632
  46.9 1.4 %copy-done.2 = bf16[16,3,2,64,128]{4,3,2,1,0:T(8,128)(2,1)S(1)} copy-done((bf16[16,3,2,64,128]{4,3,2,1,0:T(8,128)(2,1)S(1)}, bf16[16,3,2,64,128]{4,3,2,1,0:T(8,128)(2,1)}, u32[]{:S(2)}) %copy-start.2) | copy-done | bytes 1572888
  48.3 45.3 %shard_map.121 = (bf16[128,2048]{1,0:T(8,128)(2,1)S(1)}, bf16[8,16,1024]{2,1,0:T(8,128)(2,1)S(1)}, bf16[16,3,2,64,128]{4,3,2,1,0:T(8,128)(2,1)S(1)}) custom-call(bf16[128,512]{1,0:T(8,128)(2,1)S(1)} %bitcast.62, bf16[512,8192]{1,0:T(8,128)(2,1)S(1)} %copy-done.1, s32[128,1]{1,0:T(8,128)S(1)} %reshape.321.keep_ref, bf16[64,128]{1,0:T(8,128)(2,1)S(1)} %reshape.286.sel_ref, ...), custom_call_target="tpu_custom_call" | custom-call | flops 1073741824 | bytes 11534336 | tf_op jit(solution)/shard_map/pallas_call | solution.py:254
  93.6 1.1 %copy-done.3 = bf16[16,3,2,64,128]{4,3,2,1,0:T(8,128)(2,1)} copy-done((bf16[16,3,2,64,128]{4,3,2,1,0:T(8,128)(2,1)}, bf16[16,3,2,64,128]{4,3,2,1,0:T(8,128)(2,1)S(1)}, u32[]{:S(2)}) %copy-start.3) | copy-done | bytes 1572888
  94.8 0.8 copy-done.4
  95.6 0.7 copy-done.5
  96.3 1.1 %reshape.283 = bf16[8,2,2,4,1024]{4,3,2,1,0:T(4,128)(2,1)S(1)} reshape(bf16[8,16,1024]{2,1,0:T(8,128)(2,1)} %copy-done.5) | data formatting | bytes 524288 | tf_op jit(solution)/shard_map/reshape | solution.py:333
  97.3 1.0 copy.111
  98.3 1.8 %reshape.284 = bf16[4,16,2048]{2,1,0:T(8,128)(2,1)} reshape(bf16[4,8,2,2,1024]{4,3,2,1,0:T(2,128)(2,1)} %copy.111) | data formatting | bytes 524288 | tf_op jit(solution)/shard_map/reshape | solution.py:334
  100.1 1.9 %copy.137 = bf16[4,32,2048]{2,1,0:T(8,128)(2,1)} copy(bf16[4,32,2048]{2,1,0:T(8,128)(2,1)} %bitcast.63) | data formatting | bytes 1048576
  102.0 2.8 %copy.138 = bf16[16,3,2,64,128]{4,3,2,1,0:T(8,128)(2,1)} copy(bf16[16,3,2,64,128]{4,3,2,1,0:T(8,128)(2,1)} %copy-done.3) | data formatting | bytes 3145728
  (28 shorter events, 0.2 us)
Async XLA Ops:
  0.6 23.1 %copy-start = (bf16[96,2,64,128]{3,2,1,0:T(8,128)(2,1)S(1)}, bf16[96,2,64,128]{3,2,1,0:T(8,128)(2,1)}, u32[]{:S(2)}) copy-start(bf16[96,2,64,128]{3,2,1,0:T(8,128)(2,1)} %param.13) | copy-start | bytes 9437188
  12.2 7.1 %copy-start.8 = (s32[32]{0:T(128)S(1)}, s32[32]{0:T(128)}, u32[]{:S(2)}) copy-start(s32[32]{0:T(128)} %param.15) | copy-start | bytes 388
  19.2 0.8 copy-start.6
  19.2 4.3 %copy-start.7 = (s32[32,3]{0,1:T(4,128)S(1)}, s32[32,3]{0,1:T(4,128)}, u32[]{:S(2)}) copy-start(s32[32,3]{0,1:T(4,128)} %param.16) | copy-start | bytes 1156
  34.3 2.4 %copy-start.11 = (s32[8,1]{0,1:T(1,128)S(1)}, s32[8,1]{0,1:T(1,128)}, u32[]{:S(2)}) copy-start(s32[8,1]{0,1:T(1,128)} %param.18) | copy-start | bytes 100
  34.3 2.6 %copy-start.9 = (s32[8]{0:T(128)S(1)}, s32[8]{0:T(128)}, u32[]{:S(2)}) copy-start(s32[8]{0:T(128)} %param.19) | copy-start | bytes 100
  34.3 2.6 %copy-start.10 = (s32[8]{0:T(128)S(1)}, s32[8]{0:T(128)}, u32[]{:S(2)}) copy-start(s32[8]{0:T(128)} %param.17) | copy-start | bytes 100
  43.5 3.4 %copy-start.1 = (bf16[512,8192]{1,0:T(8,128)(2,1)S(1)}, bf16[512,8192]{1,0:T(8,128)(2,1)}, u32[]{:S(2)}) copy-start(bf16[512,8192]{1,0:T(8,128)(2,1)} %w_ref.1) | copy-start | bytes 25165828
  46.9 1.4 %copy-start.2 = (bf16[16,3,2,64,128]{4,3,2,1,0:T(8,128)(2,1)S(1)}, bf16[16,3,2,64,128]{4,3,2,1,0:T(8,128)(2,1)}, u32[]{:S(2)}) copy-start(bf16[16,3,2,64,128]{4,3,2,1,0:T(8,128)(2,1)} %broadcast_select_fusion.pages_ref) | copy-start | bytes 4718596
  93.6 1.2 %copy-start.3 = (bf16[16,3,2,64,128]{4,3,2,1,0:T(8,128)(2,1)}, bf16[16,3,2,64,128]{4,3,2,1,0:T(8,128)(2,1)S(1)}, u32[]{:S(2)}) copy-start(bf16[16,3,2,64,128]{4,3,2,1,0:T(8,128)(2,1)S(1)} %get-tuple-element.27) | copy-start | bytes 4718596
  94.8 0.8 copy-start.4
  95.6 0.7 copy-start.5

commit v3 on v2

--- a/solution.py
+++ b/solution.py
@@ -15,43 +15,135 @@
 ROPE_BASE = 500000.0
 
 
-def rotate(query, position):
-    half = query.shape[-1] // 2
-    inverse = ROPE_BASE ** (-jnp.arange(half, dtype=jnp.float32) * 2.0 / query.shape[-1])
-    angles = position.astype(jnp.float32)[..., None] * inverse
-    angles = jnp.concatenate([angles, angles], axis=-1)
-    turned = jnp.concatenate([-query[..., half:], query[..., :half]], axis=-1)
-    return query * jnp.cos(angles) + turned * jnp.sin(angles)
-
-
-def attend(query, pages, length, fresh):
-    count = pages.shape[0]
-    depth = query.shape[-1]
-    steps_n = query.shape[0]
-    keys = pages[:, :, 0].reshape(count, -1, depth)
-    values = pages[:, :, 1].reshape(count, -1, depth)
-    scale = depth ** (-0.5)
-    older = jnp.einsum("sbgd,bld->bsgl", query, keys, preferred_element_type=jnp.float32) * scale
-    newer = (
-        jnp.einsum("sbgd,ubd->bsgu", query, fresh[:, :, 0], preferred_element_type=jnp.float32)
-        * scale
+def turns(position, depth):
+    half = depth // 2
+    inverse = ROPE_BASE ** (-jnp.arange(half, dtype=jnp.float32) * 2.0 / depth)
+    angles = position.astype(jnp.float32)[:, None] * inverse
+    cosine = jnp.cos(angles)
+    sine = jnp.sin(angles)
+    return jnp.concatenate([cosine, cosine], axis=1), jnp.concatenate([-sine, sine], axis=1)
+
+
+def attend_kernel(
+    lengths, table, slot_table, filled, hidden_ref, wq_ref, pool_ref, fresh_ref, cos_ref, sin_ref,
+    att_ref, slots_ref,
+    h_buf, w_buf, pool, query, result, h_sem, w_sem, pool_sem,
+):
+    steps = w_buf.shape[0]
+    depth = w_buf.shape[1]
+    requests, pairs, hd = query.shape
+    groups = att_ref.shape[1] // hd
+    steps_n = pairs // groups
+    page = pool.shape[2]
+    maxp = table.shape[1]
+
+    def h_copy(k):
+        return pltpu.make_async_copy(
+            hidden_ref.at[:, pl.ds(k * depth, depth)], h_buf.at[k], h_sem.at[k]
+        )
+
+    def w_copy(k):
+        return pltpu.make_async_copy(wq_ref.at[pl.ds(k * depth, depth)], w_buf.at[k], w_sem.at[k])
+
+    pool_copy = pltpu.make_async_copy(pool_ref, pool, pool_sem)
+    for k in range(steps):
+        h_copy(k).start()
+        w_copy(k).start()
+    pool_copy.start()
+    total = jnp.zeros(att_ref.shape, jnp.float32)
+    for k in range(steps):
+        h_copy(k).wait()
+        w_copy(k).wait()
+        total = total + jnp.dot(h_buf[k], w_buf[k], preferred_element_type=jnp.float32)
+    for g in range(groups):
+        head = total[:, g * hd:(g + 1) * hd]
+        head = head * cos_ref[...] + pltpu.roll(head, hd // 2, 1) * sin_ref[...]
+        for s in range(steps_n):
+            query[:, s * groups + g, :] = head[s * requests:(s + 1) * requests]
+    pool_copy.wait()
+
+    old = maxp * page
+    span = old + page
+    column = lax.broadcasted_iota(jnp.int32, (pairs, span), 1)
+    step = lax.broadcasted_iota(jnp.int32, (pairs, span), 0) // groups
+    newer = (column >= old) & (column - old <= step)
+    scale = hd ** (-0.5)
+    empty = jnp.zeros((page - fresh_ref.shape[2], hd), jnp.bfloat16)
+
+    def one(r):
+        pages = [pool[table[r, p]] for p in range(maxp)]
+        fresh = fresh_ref[r]
+        keys = jnp.concatenate([x[0] for x in pages] + [fresh[0], empty], axis=0)
+        scores = lax.dot_general(
+            query[r].astype(jnp.bfloat16), keys, (((1,), (1,)), ((), ())),
+            preferred_element_type=jnp.float32,
+        ) * scale
+        live = newer | (column < lengths[r])
+        scores = jnp.where(live, scores, -1e30)
+        weight = jnp.exp(scores - jnp.max(scores, axis=1, keepdims=True))
+        probs = (weight / jnp.sum(weight, axis=1, keepdims=True)).astype(jnp.bfloat16)
+        values = jnp.concatenate([x[1] for x in pages] + [fresh[1], empty], axis=0)
+        result[r] = jnp.dot(probs, values, preferred_element_type=jnp.float32)
+
+    unroll = 8
+
+    def several(i, carry):
+        for k in range(unroll):
+            one(i * unroll + k)
+        return carry
+
+    lax.fori_loop(0, requests // unroll, several, 0)
+
+    def slot(i, carry):
+        for p in range(maxp):
+            chosen = pool[slot_table[i, p]]
+            slots_ref[i, p] = jnp.where(filled[i] > 0, chosen, jnp.zeros_like(chosen))
+        return carry
+
+    lax.fori_loop(0, slots_ref.shape[0], slot, 0)
+    for s in range(steps_n):
+        for g in range(groups):
+            att_ref[s * requests:(s + 1) * requests, g * hd:(g + 1) * hd] = result[
+                :, s * groups + g, :
+            ].astype(jnp.bfloat16)
+
+
+def attend(hidden, query_weight, kv_pool, new_kv, cosine, sine, lengths, table, slot_table, filled):
+    steps_n, requests, width = hidden.shape
+    columns = query_weight.shape[1]
+    hd = kv_pool.shape[-1]
+    pairs = steps_n * (columns // hd)
+    fresh = jnp.transpose(new_kv, (1, 2, 0, 3))
+    fresh = jnp.pad(fresh, ((0, 0), (0, 0), (0, 16 - steps_n), (0, 0)))
+    cuts = 8
+    depth = width // cuts
+    vmem = pl.BlockSpec(memory_space=pltpu.VMEM)
+    smem = pl.BlockSpec(memory_space=pltpu.SMEM)
+    hbm = pl.BlockSpec(memory_space=pl.ANY)
+    slots = slot_table.shape[0]
+    return pl.pallas_call(
+        attend_kernel,
+        out_shape=(
+            jax.ShapeDtypeStruct((steps_n * requests, columns), jnp.bfloat16),
+            jax.ShapeDtypeStruct((slots, table.shape[1]) + kv_pool.shape[1:], kv_pool.dtype),
+        ),
+        in_specs=[smem] * 4 + [hbm, hbm, hbm, vmem, vmem, vmem],
+        out_specs=(vmem, vmem),
+        scratch_shapes=[
+            pltpu.VMEM((cuts, steps_n * requests, depth), jnp.bfloat16),
+            pltpu.VMEM((cuts, depth, columns), jnp.bfloat16),
+            pltpu.VMEM(kv_pool.shape, kv_pool.dtype),
+            pltpu.VMEM((requests, pairs, hd), jnp.float32),
+            pltpu.VMEM((requests, pairs, hd), jnp.float32),
+            pltpu.SemaphoreType.DMA((cuts,)),
+            pltpu.SemaphoreType.DMA((cuts,)),
+            pltpu.SemaphoreType.DMA,
+        ],
+        compiler_params=pltpu.CompilerParams(vmem_limit_bytes=40 * 1024 * 1024),
+    )(
+        lengths, table, slot_table, filled, hidden.reshape(-1, width), query_weight, kv_pool, fresh,
+        cosine, sine,
     )
-    live = jnp.arange(keys.shape[1], dtype=jnp.int32)[None, :] < length[:, None]
-    older = jnp.where(live[:, None, None, :], older, -1e30)
-    step_ids = jnp.arange(steps_n, dtype=jnp.int32)
-    causal = step_ids[None, :] <= step_ids[:, None]
-    newer = jnp.where(causal[None, :, None, :], newer, -1e30)
-    top = jnp.maximum(jnp.max(older, axis=-1), jnp.max(newer, axis=-1))[..., None]
-    older_w = jnp.exp(older - top)
-    newer_w = jnp.exp(newer - top)
-    total = (jnp.sum(older_w, axis=-1) + jnp.sum(newer_w, axis=-1))[..., None]
-    older_p = (older_w / total).astype(jnp.bfloat16)
-    newer_p = (newer_w / total).astype(jnp.bfloat16)
-    result = jnp.einsum("bsgl,bld->sbgd", older_p, values, preferred_element_type=jnp.float32)
-    result = result + jnp.einsum(
-        "bsgu,ubd->sbgd", newer_p, fresh[:, :, 1], preferred_element_type=jnp.float32
-    )
-    return result.astype(jnp.bfloat16).reshape(steps_n, count, -1)
 
 
 MESH = pl.DeviceIdType.MESH
@@ -307,15 +399,11 @@
     filled = jnp.sum(chosen, axis=1)
     slot_resume = jnp.where(filled > 0, jnp.sum(chosen * resume[None, :], axis=1), steps_n)
     slot_table = jnp.sum(chosen[:, :, None] * page_table[mig_req][None], axis=1)
-    slot_pages = jnp.where(
-        (filled > 0)[:, None, None, None, None], kv_pool[slot_table], jnp.zeros((), kv_pool.dtype)
+    position = lengths[None, :] + jnp.arange(steps_n, dtype=jnp.int32)[:, None]
+    cosine, sine = turns(position.reshape(-1), HD)
+    attended, slot_pages = attend(
+        hidden, query_weight, kv_pool, new_kv, cosine, sine, lengths, page_table, slot_table, filled
     )
-    query = jnp.dot(hidden.reshape(-1, width), query_weight, preferred_element_type=jnp.float32)
-    query = query.reshape(steps_n, local_rows, GROUP, HD)
-    position = lengths[None, :] + jnp.arange(steps_n, dtype=jnp.int32)[:, None]
-    rotated = rotate(query, position[:, :, None]).astype(jnp.bfloat16)
-    pages = kv_pool[page_table]
-    attended = attend(rotated, pages, lengths, new_kv)
     hit = mig_req[:, None] == jnp.arange(local_rows, dtype=jnp.int32)[None, :]
     moved = jnp.min(jnp.where(hit, resume[:, None], steps_n), axis=0)
     step_ids = jnp.arange(steps_n, dtype=jnp.int32)[:, None]
@@ -327,7 +415,7 @@
     select = (goes & same_step[None])[:, :, :, None] & picked[:, None, None, :]
     select = select.astype(jnp.bfloat16).reshape(instances * CAP * steps_n, steps_n * local_rows)
     home, arrive, got_pages = project(
-        attended.reshape(-1, attended.shape[-1]), output_weight, keep, select, slot_pages
+        attended, output_weight, keep, select, slot_pages
     )
     home = home.reshape(steps_n, local_rows, -1)
     arrive = arrive.reshape(instances, 2, CAP, steps_n, -1)

time: 105 us -> 82.4 us (0.78)
  local copies, waits for them, and re-layouts: 39.2 us -> 13.4 us
  Pallas kernels: 45.3 us -> 62.5 us
  matrix products: 13 us -> 0 us
    pallas_call x0 -> x1, Pallas kernels: none -> 17.1 us  [attend(): pl.pallas_call(attend_kernel, out_shape=(jax.ShapeDtypeStruct((steps_n *...]
    dot_general x5 -> x0, matrix products: 13 us -> none  [the longest x1 6.95 us: local(): jnp.dot(hidden.reshape(-1, width), query_weight, preferred_element_type=j...]
    dot_general x2 -> x0, local copies, waits for them, and re-layouts: 12.7 us -> none  [the longest x1 11.6 us: local(): jnp.dot(hidden.reshape(-1, width), query_weight, preferred_element_type=j...]
    gather x2 -> x0, local copies, waits for them, and re-layouts: 4.66 us -> none  [the longest x1 2.72 us: local(): pages = kv_pool[page_table]]
    slice x2 -> x0, local copies, waits for them, and re-layouts: 3.82 us -> none  [the longest x1 3.73 us: attend(): keys = pages[:, :, 0].reshape(count, -1, depth)]
    select_n x3 -> x0, other arithmetic: 2.73 us -> none  [the longest x1 2.72 us: local(): jnp.where((filled > 0)[:, None, None, None, None], kv_pool[slot_table], j...]
    reduce_sum x2 -> x0, other arithmetic: 1.57 us -> none  [attend(): total = (jnp.sum(older_w, axis=-1) + jnp.sum(newer_w, axis=-1))[..., None]]
    unnamed x28 -> x12, local copies, waits for them, and re-layouts: 12.3 us -> 11.1 us
where the time goes in v3:
time: 82.4 us; the launch traced here: 82 us
  Pallas kernels  62.5 us (76%)
  local copies, waits for them, and re-layouts  13.4 us (16%)
  other arithmetic  5.38 us (7%)
    pallas_call x1, Pallas kernels, project(): pl.pallas_call(functools.partial(project_kernel, n, ni, chunks), out_shap...  45.3 us
    pallas_call x1, Pallas kernels, attend(): pl.pallas_call(attend_kernel, out_shape=(jax.ShapeDtypeStruct((steps_n *...  17.1 us
    unnamed x12, local copies, waits for them, and re-layouts  11.1 us

profile of v3, /device:TPU:17, one launch (start us, length us, event | category | flops | bytes accessed | tf_op | source)
XLA Modules:
  0.0 82.0 jit_solution(7151867440630988653)
XLA Ops:
  0.6 0.9 %convert_reduce_fusion = s32[8]{0:T(128)S(1)} fusion(s32[8]{0:T(128)} %bitcast.12), kind=kLoop, calls=%fused_computation.18 | loop fusion | flops 312 | bytes 64 | tf_op jit(solution)/shard_map/reduce_sum | solution.py:394
  1.5 0.7 multiply_add_fusion
  2.2 0.8 select_reduce_fusion.2
  3.0 0.7 compare_select_fusion
  3.7 0.8 select_reduce_fusion.1
  4.4 0.1 fusion.1
  4.5 0.1 iota_compare_fusion.1
  4.6 0.7 add_convert_fusion
  5.2 0.1 convert_element_type.45
  5.3 0.1 fusion.2
  5.4 0.1 broadcast_and_fusion
  5.5 0.8 copy.21.table
  6.3 0.6 gather_fusion
  6.8 0.1 copy.19
  6.9 0.1 multiply_reduce_fusion
  7.0 0.1 copy.22.slot_table
  7.1 0.1 and_convert_fusion
  7.2 0.1 reshape.189.sel_ref
  7.3 0.1 reshape.199.keep_ref
  7.4 0.9 %copy.26 = bf16[4,32,2,128]{3,0,2,1:T(4,128)(2,1)S(1)} copy(bf16[4,32,2,128]{3,2,1,0:T(2,128)(2,1)} %param.14) | data formatting | bytes 131072 | tf_op args[4]
  8.3 0.3 fusion
  8.7 0.1 pad_maximum_fusion
  8.8 0.0 copy-start.1
  8.8 1.9 %copy-done.1 = bf16[96,2,64,128]{3,2,1,0:T(8,128)(2,1)S(1)} copy-done((bf16[96,2,64,128]{3,2,1,0:T(8,128)(2,1)S(1)}, bf16[96,2,64,128]{3,2,1,0:T(8,128)(2,1)}, u32[]{:S(2)}) %copy-start.1) | copy-done | bytes 3145752
  10.7 0.0 copy-start.2
  10.7 1.6 %copy-done.2 = bf16[4,32,8192]{2,1,0:T(8,128)(2,1)S(1)} copy-done((bf16[4,32,8192]{2,1,0:T(8,128)(2,1)S(1)}, bf16[4,32,8192]{2,1,0:T(8,128)(2,1)}, u32[]{:S(2)}) %copy-start.2) | copy-done | bytes 2097176
  12.3 0.0 copy-start.3
  12.3 0.7 copy-done.3
  12.9 17.1 %shard_map.121 = (bf16[128,512]{1,0:T(8,128)(2,1)S(1)}, bf16[16,3,2,64,128]{4,3,2,1,0:T(8,128)(2,1)S(1)}) custom-call(s32[32]{0:T(128)S(1)} %copy-done.3, s32[32,3]{1,0:T(8,128)S(1)} %copy.21.table, s32[16,3]{1,0:T(8,128)S(1)} %copy.22.slot_table, s32[16]{0:T(128)S(1)} %get-tuple-element.14.filled, bf16[128,8192]{1,0:T(8,128)(2,1)S(1)} %bitcast.8, ...), custom_call_target="tpu_custom_call" | custom-call | tf_op jit(solution)/shard_map/pallas_call | solution.py:124
  30.1 0.0 copy-start
  30.1 3.4 %copy-done = bf16[512,8192]{1,0:T(8,128)(2,1)S(1)} copy-done((bf16[512,8192]{1,0:T(8,128)(2,1)S(1)}, bf16[512,8192]{1,0:T(8,128)(2,1)}, u32[]{:S(2)}) %copy-start) | copy-done | bytes 8388632
  33.5 45.3 %shard_map.122 = (bf16[128,2048]{1,0:T(8,128)(2,1)S(1)}, bf16[8,16,1024]{2,1,0:T(8,128)(2,1)S(1)}, bf16[16,3,2,64,128]{4,3,2,1,0:T(8,128)(2,1)S(1)}) custom-call(bf16[128,512]{1,0:T(8,128)(2,1)S(1)} %get-tuple-element.8.att_ref, bf16[512,8192]{1,0:T(8,128)(2,1)S(1)} %copy-done, s32[128,1]{1,0:T(8,128)S(1)} %reshape.199.keep_ref, ...), custom_call_target="tpu_custom_call" | custom-call | flops 1073741824 | bytes 11534336 | tf_op jit(solution)/shard_map/pallas_call | solution.py:346
  78.8 0.1 reshape.186
  78.9 0.3 copy.24
  79.2 0.9 %reshape.187 = bf16[4,16,2048]{2,1,0:T(8,128)(2,1)} reshape(bf16[4,8,2,2,1024]{4,3,2,1,0:T(2,128)(2,1)S(1)} %copy.24) | data formatting | bytes 524288 | tf_op jit(solution)/shard_map/reshape | solution.py:422
  80.1 0.8 copy.29
  80.9 1.1 %copy.30 = bf16[16,3,2,64,128]{4,3,2,1,0:T(8,128)(2,1)} copy(bf16[16,3,2,64,128]{4,3,2,1,0:T(8,128)(2,1)S(1)} %get-tuple-element.26) | data formatting | bytes 3145728
  (7 shorter events, 0.1 us)
Async XLA Ops:
  8.8 1.9 %copy-start.1 = (bf16[96,2,64,128]{3,2,1,0:T(8,128)(2,1)S(1)}, bf16[96,2,64,128]{3,2,1,0:T(8,128)(2,1)}, u32[]{:S(2)}) copy-start(bf16[96,2,64,128]{3,2,1,0:T(8,128)(2,1)} %pool_ref.1) | copy-start | bytes 9437188
  10.7 1.6 %copy-start.2 = (bf16[4,32,8192]{2,1,0:T(8,128)(2,1)S(1)}, bf16[4,32,8192]{2,1,0:T(8,128)(2,1)}, u32[]{:S(2)}) copy-start(bf16[4,32,8192]{2,1,0:T(8,128)(2,1)} %param.10) | copy-start | bytes 6291460
  12.3 0.7 copy-start.3
  30.1 3.4 %copy-start = (bf16[512,8192]{1,0:T(8,128)(2,1)S(1)}, bf16[512,8192]{1,0:T(8,128)(2,1)}, u32[]{:S(2)}) copy-start(bf16[512,8192]{1,0:T(8,128)(2,1)} %w_ref.1) | copy-start | bytes 25165828

commit v4 on v1

v4 whole, which is shorter than its diff:
```python
import functools

import jax
import jax.numpy as jnp
from jax import lax
from jax.experimental import pallas as pl
from jax.experimental.pallas import tpu as pltpu
from jax.sharding import PartitionSpec as P

HD = 128
CAP = 2
HALVES = 2


ROPE_BASE = 500000.0

MESH = pl.DeviceIdType.MESH


def turns(position, depth):
    half = depth // 2
    inverse = ROPE_BASE ** (-jnp.arange(half, dtype=jnp.float32) * 2.0 / depth)
    angles = position.astype(jnp.float32)[:, None] * inverse
    cosine = jnp.cos(angles)
    sine = jnp.sin(angles)
    return jnp.concatenate([cosine, cosine], axis=1), jnp.concatenate([-sine, sine], axis=1)


def layer_kernel(
    n, ni, chunks,
    lengths, table, mig_req, mig_dest, resume,
    hidden_ref, wq_ref, pool_ref, wo_ref, fresh_ref, cos_ref, sin_ref,
    home_ref, arrive_ref, got_ref,
    h_buf, wq_buf, pool, wo_buf, query, result, att, part, up_in, down_in, up_out, down_out,
    slots, select, leave,
    h_sem, wq_sem, pool_sem, wo_sem,
    up_send, up_recv, down_send, down_recv, page_send, page_recv, row_send, row_recv, own_sem,
):
    z = lax.axis_index("tp")
    me = lax.axis_index("inst")
    cuts, depth, columns = wq_buf.shape
    requests, pairs, hd = query.shape
    groups = columns // hd
    steps_n = pairs // groups
    page = pool.shape[2]
    maxp = table.shape[0]
    leaving = mig_req.shape[0]
    some = requests // HALVES
    rows, width = part.shape[2:]
    hops = (n - 1) * chunks
    low = z < n // 2

    def h_copy(k):
        return pltpu.make_async_copy(
            hidden_ref.at[:, pl.ds(k * depth, depth)], h_buf.at[k], h_sem.at[k]
        )

    def wq_copy(k):
        return pltpu.make_async_copy(
            wq_ref.at[pl.ds(k * depth, depth)], wq_buf.at[k], wq_sem.at[k]
        )

    def block_of(k):
        return jnp.where(low, n - 1 - k // chunks, k // chunks)

    def wo_copy(k):
        column = (block_of(k) * chunks + k % chunks) * width
        return pltpu.make_async_copy(
            wo_ref.at[:, pl.ds(pl.multiple_of(column, width), width)], wo_buf.at[k], wo_sem.at[k]
        )

    pool_copy = pltpu.make_async_copy(pool_ref, pool, pool_sem)
    pool_copy.start()
    for k in range(cuts):
        h_copy(k).start()
        wq_copy(k).start()
    for k in range(n * chunks):
        wo_copy(k).start()

    barrier = pltpu.get_barrier_semaphore()
    for k in range(1, ni):
        pl.semaphore_signal(
            barrier, inc=1, device_id={"inst": lax.rem(me + k, ni)}, device_id_type=MESH
        )

    @pl.when(z > 0)
    def _():
        pl.semaphore_signal(barrier, inc=1, device_id={"tp": z - 1}, device_id_type=MESH)

    @pl.when(z < n - 1)
    def _():
        pl.semaphore_signal(barrier, inc=1, device_id={"tp": z + 1}, device_id_type=MESH)

    slot_rows = CAP * steps_n
    shape = (slot_rows, HALVES * rows)
    slot_row = lax.broadcasted_iota(jnp.int32, shape, 0)
    row = lax.broadcasted_iota(jnp.int32, shape, 1)
    slot_step = slot_row % steps_n
    row_request = (row // rows) * some + row % some
    row_step = (row % rows) // some

    pool_copy.wait()

    def fill(d, carry):
        count = jnp.int32(0)
        who = [jnp.int32(-1) for _ in range(CAP)]
        start = [jnp.int32(steps_n) for _ in range(CAP)]
        for k in range(leaving):
            match = mig_dest[k] == d
            for c in range(CAP):
                take = match & (count == c)
                who[c] = jnp.where(take, mig_req[k], who[c])
                start[c] = jnp.where(take, resume[k], start[c])
            count = count + match.astype(jnp.int32)
        chosen = jnp.full(shape, -1, jnp.int32)
        first = jnp.full(shape, steps_n, jnp.int32)
        for c in range(CAP):
            chosen = jnp.where(slot_row // steps_n == c, who[c], chosen)
            first = jnp.where(slot_row // steps_n == c, start[c], first)
            for p in range(maxp):
                pages = pool[table[p, jnp.maximum(who[c], 0)]]
                slots[d * CAP + c, p] = jnp.where(who[c] >= 0, pages, jnp.zeros_like(pages))
        hit = (row_request == chosen) & (row_step == slot_step) & (slot_step >= first)
        select[d] = hit.astype(jnp.float32)
        return carry

    lax.fori_loop(0, ni, fill, 0)

    pl.semaphore_wait(barrier, ni - 1 + (z > 0).astype(jnp.int32) + (z < n - 1).astype(jnp.int32))

    def page_copy(k):
        to = lax.rem(me + k, ni)
        return pltpu.make_async_remote_copy(
            src_ref=slots.at[pl.ds(to * CAP, CAP)],
            dst_ref=got_ref.at[pl.ds(me * CAP, CAP)],
            send_sem=page_send.at[k],
            recv_sem=page_recv.at[k],
            device_id={"inst": to},
            device_id_type=MESH,
        )

    own_pages = pltpu.make_async_copy(
        slots.at[pl.ds(me * CAP, CAP)], got_ref.at[pl.ds(me * CAP, CAP)], own_sem.at[0]
    )
    for k in range(1, ni):
        page_copy(k).start()
    own_pages.start()

    total = jnp.zeros((h_buf.shape[1], columns), jnp.float32)
    for k in range(cuts):
        h_copy(k).wait()
        wq_copy(k).wait()
        total = total + jnp.dot(h_buf[k], wq_buf[k], preferred_element_type=jnp.float32)
    for g in range(groups):
        head = total[:, g * hd:(g + 1) * hd]
        head = head * cos_ref[...] + pltpu.roll(head, hd // 2, 1) * sin_ref[...]
        for s in range(steps_n):
            query[:, s * groups + g, :] = head[s * requests:(s + 1) * requests]

    old = maxp * page
    span = old + page
    column = lax.broadcasted_iota(jnp.int32, (pairs, span), 1)
    step = lax.broadcasted_iota(jnp.int32, (pairs, span), 0) // groups
    newer = (column >= old) & (column - old <= step)
    scale = hd ** (-0.5)
    empty = jnp.zeros((page - fresh_ref.shape[2], hd), jnp.bfloat16)

    def one(r):
        pages = [pool[table[p, r]] for p in range(maxp)]
        fresh = fresh_ref[r]
        keys = jnp.concatenate([x[0] for x in pages] + [fresh[0], empty], axis=0)
        scores = lax.dot_general(
            query[r].astype(jnp.bfloat16), keys, (((1,), (1,)), ((), ())),
            preferred_element_type=jnp.float32,
        ) * scale
        live = newer | (column < lengths[r])
        scores = jnp.where(live, scores, -1e30)
        weight = jnp.exp(scores - jnp.max(scores, axis=1, keepdims=True))
        probs = (weight / jnp.sum(weight, axis=1, keepdims=True)).astype(jnp.bfloat16)
        values = jnp.concatenate([x[1] for x in pages] + [fresh[1], empty], axis=0)
        result[r] = jnp.dot(probs, values, preferred_element_type=jnp.float32)

    def up_copy(j):
        return pltpu.make_async_remote_copy(
            src_ref=up_out.at[j], dst_ref=up_in.at[j],
            send_sem=up_send.at[j], recv_sem=up_recv.at[j],
            device_id={"tp": jnp.minimum(z + 1, n - 1)}, device_id_type=MESH,
        )

    def down_copy(j):
        return pltpu.make_async_remote_copy(
            src_ref=down_out.at[j], dst_ref=down_in.at[j],
            send_sem=down_send.at[j], recv_sem=down_recv.at[j],
            device_id={"tp": jnp.maximum(z - 1, 0)}, device_id_type=MESH,
        )

    unroll = 8
    for h in range(HALVES):

        def several(i, carry, h=h):
            for k in range(unroll):
                one(h * some + i * unroll + k)
            return carry

        lax.fori_loop(0, some // unroll, several, 0)
        for s in range(steps_n):
            for g in range(groups):
                att[h, s * some:(s + 1) * some, g * hd:(g + 1) * hd] = result[
                    h * some:(h + 1) * some, s * groups + g, :
                ].astype(jnp.bfloat16)

        def compute(k, carry, h=h):
            if h == 0:
                wo_copy(k).wait()
            value = jnp.dot(att[h], wo_buf[k], preferred_element_type=jnp.float32)
            part[h, block_of(k) * chunks + k % chunks] = value

            @pl.when((z == 0) & (k < hops))
            def _():
                up_out[h * hops + k] = value.astype(jnp.bfloat16)
                up_copy(h * hops + k).start()

            @pl.when((z == n - 1) & (k < hops))
            def _():
                down_out[h * hops + k] = value.astype(jnp.bfloat16)
                down_copy(h * hops + k).start()

            return carry

        lax.fori_loop(0, n * chunks, compute, 0)

    up_lag = jnp.maximum(z - 1, 0)
    down_lag = jnp.maximum(n - 2 - z, 0)
    for h in range(HALVES):

        def relay(j, carry, h=h):
            ju = j - up_lag
            jd = j - down_lag

            @pl.when((z > 0) & (ju >= 0) & (ju < (n - z) * chunks))
            def _():
                up_copy(h * hops + ju).wait_recv()
                spot = (n - 1 - ju // chunks) * chunks + ju % chunks
                value = part[h, spot] + up_in[h * hops + ju].astype(jnp.float32)

                @pl.when(ju < (n - 1 - z) * chunks)
                def _():
                    up_out[h * hops + ju] = value.astype(jnp.bfloat16)
                    up_copy(h * hops + ju).start()

                @pl.when(ju >= (n - 1 - z) * chunks)
                def _():
                    part[h, spot] = value

            @pl.when((z < n - 1) & (jd >= 0) & (jd < (z + 1) * chunks))
            def _():
                down_copy(h * hops + jd).wait_recv()
                value = part[h, jd] + down_in[h * hops + jd].astype(jnp.float32)

                @pl.when(jd < z * chunks)
                def _():
                    down_out[h * hops + jd] = value.astype(jnp.bfloat16)
                    down_copy(h * hops + jd).start()

                @pl.when(jd >= z * chunks)
                def _():
                    part[h, jd] = value

            return carry

        lax.fori_loop(0, hops + n - 2, relay, 0)

    selection = select[...].reshape(ni * slot_rows, HALVES * rows).astype(jnp.bfloat16)
    lane_row = lax.broadcasted_iota(jnp.int32, (rows, hd), 0)
    half = chunks // 2
    stays = []
    for h in range(HALVES):
        kept = jnp.ones((rows, hd), jnp.int32)
        for k in range(leaving):
            gone = (lane_row % some + h * some == mig_req[k]) & (lane_row // some >= resume[k])
            kept = jnp.where(gone, 0, kept)
        stays.append(jnp.concatenate([kept] * (width // hd), axis=1))
    for c in range(half):
        pieces = []
        for d in (c, c + half):
            mines = []
            for h in range(HALVES):
                mine = part[h, z * chunks + d].astype(jnp.bfloat16)
                mines.append(mine)
                kept = jnp.where(stays[h] > 0, mine.astype(jnp.float32), 0.0).astype(jnp.bfloat16)
                for s in range(steps_n):
                    home_ref[
                        s * requests + h * some:s * requests + (h + 1) * some,
                        d * width:(d + 1) * width,
                    ] = kept[s * some:(s + 1) * some]
            moved = jnp.dot(
                selection, jnp.concatenate(mines, axis=0), preferred_element_type=jnp.float32
            )
            pieces.append(moved.reshape(ni, slot_rows, width))
        leave[:, :, c * width:(c + 1) * width] = jnp.concatenate(pieces, axis=1).astype(jnp.bfloat16)

    def row_copy(k):
        to = lax.rem(me + k, ni)
        return pltpu.make_async_remote_copy(
            src_ref=leave.at[to],
            dst_ref=arrive_ref.at[me],
            send_sem=row_send.at[k],
            recv_sem=row_recv.at[k],
            device_id={"inst": to},
            device_id_type=MESH,
        )

    own_rows = pltpu.make_async_copy(leave.at[me], arrive_ref.at[me], own_sem.at[1])
    for k in range(1, ni):
        row_copy(k).start()
    own_rows.start()

    for h in range(HALVES):

        def drain(j, carry, h=h):
            @pl.when((z < n - 1) & (j < (n - 1 - z) * chunks))
            def _():
                up_copy(h * hops + j).wait_send()

            @pl.when((z > 0) & (j < z * chunks))
            def _():
                down_copy(h * hops + j).wait_send()

            return carry

        lax.fori_loop(0, hops, drain, 0)
    for k in range(1, ni):
        page_copy(k).wait()
    own_pages.wait()
    for k in range(1, ni):
        row_copy(k).wait()
    own_rows.wait()


def local(
    hidden,
    query_weight,
    output_weight,
    kv_pool,
    new_kv,
    lengths,
    page_table,
    mig_req,
    mig_dest,
    resume,
):
    steps_n, requests, width = hidden.shape
    n = lax.axis_size("tp")
    ni = lax.axis_size("inst")
    columns = query_weight.shape[1]
    pairs = steps_n * (columns // HD)
    maxp = page_table.shape[1]
    all_rows = steps_n * requests
    rows = all_rows // HALVES
    share = output_weight.shape[1] // n
    chunk = min(1024, share // 2)
    chunks = share // chunk
    hops = (n - 1) * chunks
    slot_rows = CAP * steps_n
    position = lengths[None, :] + jnp.arange(steps_n, dtype=jnp.int32)[:, None]
    cosine, sine = turns(position.reshape(-1), HD)
    fresh = jnp.transpose(new_kv, (1, 2, 0, 3))
    fresh = jnp.pad(fresh, ((0, 0), (0, 0), (0, 16 - steps_n), (0, 0)))
    cuts = 8
    vmem = pl.BlockSpec(memory_space=pltpu.VMEM)
    smem = pl.BlockSpec(memory_space=pltpu.SMEM)
    hbm = pl.BlockSpec(memory_space=pl.ANY)
    relay = pltpu.VMEM((HALVES * hops, rows, chunk), jnp.bfloat16)
    dma = pltpu.SemaphoreType.DMA
    bf16, f32 = jnp.bfloat16, jnp.float32
    slot_shape = (ni * CAP, maxp) + kv_pool.shape[1:]
    home, arrive, got_pages = pl.pallas_call(
        functools.partial(layer_kernel, n, ni, chunks),
        out_shape=(
            jax.ShapeDtypeStruct((all_rows, share), bf16),
            jax.ShapeDtypeStruct((ni, 2 * slot_rows, share // 2), bf16),
            jax.ShapeDtypeStruct(slot_shape, bf16),
        ),
        in_specs=[smem] * 5 + [hbm] * 4 + [vmem] * 3,
        out_specs=(vmem, hbm, hbm),
        scratch_shapes=[
            pltpu.VMEM((cuts, all_rows, width // cuts), bf16),
            pltpu.VMEM((cuts, width // cuts, columns), bf16),
            pltpu.VMEM(kv_pool.shape, bf16),
            pltpu.VMEM((n * chunks, columns, chunk), bf16),
            pltpu.VMEM((requests, pairs, HD), f32),
            pltpu.VMEM((requests, pairs, HD), f32),
            pltpu.VMEM((HALVES, rows, columns), bf16),
            pltpu.VMEM((HALVES, n * chunks, rows, chunk), f32),
            relay, relay, relay, relay,
            pltpu.VMEM(slot_shape, bf16),
            pltpu.VMEM((ni, slot_rows, all_rows), f32),
            pltpu.VMEM((ni, 2 * slot_rows, share // 2), bf16),
            dma((cuts,)), dma((cuts,)), dma, dma((n * chunks,)),
            dma((HALVES * hops,)), dma((HALVES * hops,)), dma((HALVES * hops,)), dma((HALVES * hops,)),
            dma((ni,)), dma((ni,)), dma((ni,)), dma((ni,)), dma((2,)),
        ],
        compiler_params=pltpu.CompilerParams(
            collective_id=0, has_side_effects=True, vmem_limit_bytes=60 * 1024 * 1024
        ),
    )(
        lengths, page_table.T, mig_req, mig_dest.reshape(-1), resume,
        hidden.reshape(-1, width), query_weight, kv_pool, output_weight, fresh, cosine, sine,
    )
    home = home.reshape(steps_n, requests, -1)
    arrive = arrive.reshape(ni, 2, CAP, steps_n, -1)
    arrival = jnp.transpose(arrive, (3, 0, 2, 1, 4)).reshape(steps_n, ni * CAP, -1)
    return (home, arrival, got_pages)


def solution(mesh):
    in_specs = (
        P(None, "inst", None),
        P(None, "tp"),
        P("tp", None),
        P("inst", None, None, "tp"),
        P(None, "inst", None, "tp"),
        P("inst"),
        P("inst", None),
        P("inst"),
        P("inst", None),
        P("inst"),
    )
    out_specs = (P(None, "inst", "tp"), P(None, "inst", "tp"), P("inst", None, None, None, "tp"))
    return jax.shard_map(local, mesh=mesh, in_specs=in_specs, out_specs=out_specs, check_vma=False)
```

time: 136 us -> 75.3 us (0.55)
  Pallas kernels: 0 us -> 65.6 us
  waiting for transfers between devices: 53.6 us -> 0 us
  local copies, waits for them, and re-layouts: 33.3 us -> 7.07 us
  matrix products: 17.7 us -> 0 us
  starting transfers between devices: 14.8 us -> 0 us
  other arithmetic: 14.5 us -> 1.74 us
    pallas_call x0 -> x1, Pallas kernels: none -> 65.6 us  [local(): pl.pallas_call(functools.partial(layer_kernel, n, ni, chunks), out_shape=...]
    all_to_all x3 -> x0, waiting for transfers between devices: 53.6 us -> none  [the longest x1 48.6 us: local(): got = lax.all_to_all(parts, 'tp', split_axis=0, concat_axis=0, tiled=True)]
    dot_general x6 -> x0, matrix products: 17.7 us -> none  [the longest x1 6.96 us: local(): jnp.dot(hidden.reshape(-1, width), query_weight, preferred_element_type=j...]
    all_to_all x3 -> x0, starting transfers between devices: 14.8 us -> none  [the longest x1 5.61 us: local(): got = lax.all_to_all(parts, 'tp', split_axis=0, concat_axis=0, tiled=True)]
    dot_general x2 -> x0, local copies, waits for them, and re-layouts: 12.5 us -> none  [the longest x1 11.4 us: local(): jnp.dot(hidden.reshape(-1, width), query_weight, preferred_element_type=j...]
    gather x5 -> x0, local copies, waits for them, and re-layouts: 7.1 us -> none  [the longest x1 2.72 us: local(): pages = kv_pool[page_table]]
    reduce_sum x6 -> x0, other arithmetic: 6.34 us -> none  [the longest x1 2.92 us: local(): mine = jnp.sum(got.astype(jnp.float32), axis=0).astype(jnp.bfloat16)]
    select_n x8 -> x0, other arithmetic: 6.23 us -> none  [the longest x1 2.73 us: local(): jnp.where((filled > 0)[:, None, None, None, None], kv_pool[slot_table], j...]
  transfers between devices with their start and end apart: 3 -> 0, of which waited for: 2 -> 0; matrix products, arithmetic and copies ran while one was open for 33% -> 0% of each run, Pallas kernels for 0% -> 0%
where the time goes in v4:
time: 75.3 us; the launch traced here: 75.1 us
  Pallas kernels  65.6 us (87%)
  local copies, waits for them, and re-layouts  7.07 us (9%)
  other arithmetic  1.74 us (2%)
    pallas_call x1, Pallas kernels, local(): pl.pallas_call(functools.partial(layer_kernel, n, ni, chunks), out_shape=...  65.6 us
    unnamed x5, local copies, waits for them, and re-layouts  3.92 us

profile of v4, /device:TPU:0, one launch (start us, length us, event | category | flops | bytes accessed | tf_op | source)
XLA Modules:
  0.0 75.1 jit_solution(8020583859982188943)
XLA Ops:
  0.6 0.7 add_convert_fusion
  1.3 0.1 convert_element_type.13
  1.4 0.9 %copy.16 = bf16[4,32,2,128]{3,0,2,1:T(4,128)(2,1)S(1)} copy(bf16[4,32,2,128]{3,2,1,0:T(2,128)(2,1)} %param.14) | data formatting | bytes 131072 | tf_op args[4]
  2.3 0.3 fusion
  2.6 0.8 %pad_maximum_fusion = (f32[128,128]{1,0:T(8,128)}, f32[128,128]{1,0:T(8,128)}) fusion(f32[128,64]{1,0:T(8,128)S(1)} %get-tuple-element.11, f32[128,64]{1,0:T(8,128)S(1)} %get-tuple-element.10, f32[128,64]{1,0:T(8,128)S(1)} %get-tuple-element.9), kind=kLoop, calls=%fused_computation.2 | loop fusion | flops 32768 | bytes 229376 | tf_op jit(solution)/shard_map/concatenate | solution.py:26
  3.4 0.7 pad.4.fresh_ref
  4.1 65.6 %shard_map.121 = (bf16[128,2048]{1,0:T(8,128)(2,1)}, bf16[8,16,1024]{2,1,0:T(8,128)(2,1)}, bf16[16,3,2,64,128]{4,3,2,1,0:T(8,128)(2,1)}) custom-call(s32[32]{0:T(128)} %lengths.1, s32[3,32]{1,0:T(4,128)} %bitcast.12, s32[8]{0:T(128)} %mig_req.1, s32[8]{0:T(128)} %bitcast.13, s32[8]{0:T(128)} %resume.1, bf16[128,8192]{1,0:T(8,128)(2,1)} %bitcast.8, ...), custom_call_target="tpu_custom_call" | custom-call | tf_op jit(solution)/shard_map/pallas_call | solution.py:377
  69.7 0.0 copy-start
  69.7 1.2 %reshape.46 = bf16[8,2,2,4,1024]{4,3,2,1,0:T(4,128)(2,1)S(1)} reshape(bf16[8,16,1024]{2,1,0:T(8,128)(2,1)} %get-tuple-element.7) | data formatting | bytes 524288 | tf_op jit(solution)/shard_map/reshape | solution.py:411
  70.9 0.3 copy.14
  71.1 0.9 %reshape.47 = bf16[4,16,2048]{2,1,0:T(8,128)(2,1)} reshape(bf16[4,8,2,2,1024]{4,3,2,1,0:T(2,128)(2,1)S(1)} %copy.14) | data formatting | bytes 524288 | tf_op jit(solution)/shard_map/reshape | solution.py:412
  72.0 1.9 %copy.19 = bf16[4,32,2048]{2,1,0:T(8,128)(2,1)} copy(bf16[4,32,2048]{2,1,0:T(8,128)(2,1)} %bitcast.10) | data formatting | bytes 1048576
  73.9 0.0 copy-done
  73.9 1.1 %copy.20 = bf16[16,3,2,64,128]{4,3,2,1,0:T(8,128)(2,1)} copy(bf16[16,3,2,64,128]{4,3,2,1,0:T(8,128)(2,1)S(1)} %copy-done) | data formatting | bytes 3145728
  (1 shorter events, 0.0 us)
Async XLA Ops:
  69.7 4.2 %copy-start = (bf16[16,3,2,64,128]{4,3,2,1,0:T(8,128)(2,1)S(1)}, bf16[16,3,2,64,128]{4,3,2,1,0:T(8,128)(2,1)}, u32[]{:S(2)}) copy-start(bf16[16,3,2,64,128]{4,3,2,1,0:T(8,128)(2,1)} %get-tuple-element.19) | copy-start | bytes 4718596

commit v5 on v4

--- a/solution.py
+++ b/solution.py
@@ -32,7 +32,7 @@
     hidden_ref, wq_ref, pool_ref, wo_ref, fresh_ref, cos_ref, sin_ref,
     home_ref, arrive_ref, got_ref,
     h_buf, wq_buf, pool, wo_buf, query, result, att, part, up_in, down_in, up_out, down_out,
-    slots, select, leave,
+    slots, select, leave, landed, fresh,
     h_sem, wq_sem, pool_sem, wo_sem,
     up_send, up_recv, down_send, down_recv, page_send, page_recv, row_send, row_recv, own_sem,
 ):
@@ -142,10 +142,6 @@
     own_pages = pltpu.make_async_copy(
         slots.at[pl.ds(me * CAP, CAP)], got_ref.at[pl.ds(me * CAP, CAP)], own_sem.at[0]
     )
-    for k in range(1, ni):
-        page_copy(k).start()
-    own_pages.start()
-
     total = jnp.zeros((h_buf.shape[1], columns), jnp.float32)
     for k in range(cuts):
         h_copy(k).wait()
@@ -157,28 +153,53 @@
         for s in range(steps_n):
             query[:, s * groups + g, :] = head[s * requests:(s + 1) * requests]
 
+    fresh[...] = jnp.zeros_like(fresh)
+    for u in range(steps_n):
+        for kind in range(2):
+            fresh[kind, :, u, :] = fresh_ref[
+                u * requests:(u + 1) * requests, kind * hd:(kind + 1) * hd
+            ].astype(jnp.float32)
+
+    batch = 8
     old = maxp * page
     span = old + page
-    column = lax.broadcasted_iota(jnp.int32, (pairs, span), 1)
-    step = lax.broadcasted_iota(jnp.int32, (pairs, span), 0) // groups
+    column = lax.broadcasted_iota(jnp.int32, (batch * pairs, span), 1)
+    step = (lax.broadcasted_iota(jnp.int32, (batch * pairs, span), 0) % pairs) // groups
     newer = (column >= old) & (column - old <= step)
     scale = hd ** (-0.5)
-    empty = jnp.zeros((page - fresh_ref.shape[2], hd), jnp.bfloat16)
-
-    def one(r):
-        pages = [pool[table[p, r]] for p in range(maxp)]
-        fresh = fresh_ref[r]
-        keys = jnp.concatenate([x[0] for x in pages] + [fresh[0], empty], axis=0)
-        scores = lax.dot_general(
-            query[r].astype(jnp.bfloat16), keys, (((1,), (1,)), ((), ())),
-            preferred_element_type=jnp.float32,
+    empty = jnp.zeros((page - fresh.shape[2], hd), jnp.bfloat16)
+
+    def stacked(r, kind):
+        return jnp.concatenate(
+            [pool[table[p, r], kind] for p in range(maxp)]
+            + [fresh[kind, r].astype(jnp.bfloat16), empty],
+            axis=0,
+        )
+
+    def several(i, carry):
+        first = i * batch
+        scores = jnp.concatenate(
+            [
+                lax.dot_general(
+                    query[first + k].astype(jnp.bfloat16), stacked(first + k, 0),
+                    (((1,), (1,)), ((), ())), preferred_element_type=jnp.float32,
+                )
+                for k in range(batch)
+            ],
+            axis=0,
         ) * scale
-        live = newer | (column < lengths[r])
-        scores = jnp.where(live, scores, -1e30)
+        length = jnp.concatenate(
+            [jnp.full((pairs, span), lengths[first + k], jnp.int32) for k in range(batch)], axis=0
+        )
+        scores = jnp.where(newer | (column < length), scores, -1e30)
         weight = jnp.exp(scores - jnp.max(scores, axis=1, keepdims=True))
         probs = (weight / jnp.sum(weight, axis=1, keepdims=True)).astype(jnp.bfloat16)
-        values = jnp.concatenate([x[1] for x in pages] + [fresh[1], empty], axis=0)
-        result[r] = jnp.dot(probs, values, preferred_element_type=jnp.float32)
+        for k in range(batch):
+            result[first + k] = jnp.dot(
+                probs[k * pairs:(k + 1) * pairs], stacked(first + k, 1),
+                preferred_element_type=jnp.float32,
+            )
+        return carry
 
     def up_copy(j):
         return pltpu.make_async_remote_copy(
@@ -194,15 +215,8 @@
             device_id={"tp": jnp.maximum(z - 1, 0)}, device_id_type=MESH,
         )
 
-    unroll = 8
     for h in range(HALVES):
-
-        def several(i, carry, h=h):
-            for k in range(unroll):
-                one(h * some + i * unroll + k)
-            return carry
-
-        lax.fori_loop(0, some // unroll, several, 0)
+        lax.fori_loop(h * some // batch, (h + 1) * some // batch, several, 0)
         for s in range(steps_n):
             for g in range(groups):
                 att[h, s * some:(s + 1) * some, g * hd:(g + 1) * hd] = result[
@@ -228,6 +242,10 @@
             return carry
 
         lax.fori_loop(0, n * chunks, compute, 0)
+        if h == 0:
+            for k in range(1, ni):
+                page_copy(k).start()
+            own_pages.start()
 
     up_lag = jnp.maximum(z - 1, 0)
     down_lag = jnp.maximum(n - 2 - z, 0)
@@ -303,14 +321,14 @@
         to = lax.rem(me + k, ni)
         return pltpu.make_async_remote_copy(
             src_ref=leave.at[to],
-            dst_ref=arrive_ref.at[me],
+            dst_ref=landed.at[me],
             send_sem=row_send.at[k],
             recv_sem=row_recv.at[k],
             device_id={"inst": to},
             device_id_type=MESH,
         )
 
-    own_rows = pltpu.make_async_copy(leave.at[me], arrive_ref.at[me], own_sem.at[1])
+    own_rows = pltpu.make_async_copy(leave.at[me], landed.at[me], own_sem.at[1])
     for k in range(1, ni):
         row_copy(k).start()
     own_rows.start()
@@ -330,11 +348,23 @@
 
         lax.fori_loop(0, hops, drain, 0)
     for k in range(1, ni):
+        row_copy(k).wait()
+    own_rows.wait()
+    arrivals = landed[...].reshape(2 * ni * slot_rows, landed.shape[2])
+    shape = (ni * slot_rows, 2 * ni * slot_rows)
+    out_row = lax.broadcasted_iota(jnp.int32, shape, 0)
+    in_row = lax.broadcasted_iota(jnp.int32, shape, 1)
+    out_slot = out_row % (ni * CAP)
+    place = (out_slot // CAP) * 2 * slot_rows + (out_slot % CAP) * steps_n + out_row // (ni * CAP)
+    side = landed.shape[2]
+    for d in range(2):
+        order = (in_row == place + d * slot_rows).astype(jnp.float32).astype(jnp.bfloat16)
+        arrive_ref[:, d * side:(d + 1) * side] = jnp.dot(
+            order, arrivals, preferred_element_type=jnp.float32
+        ).astype(jnp.bfloat16)
+    for k in range(1, ni):
         page_copy(k).wait()
     own_pages.wait()
-    for k in range(1, ni):
-        row_copy(k).wait()
-    own_rows.wait()
 
 
 def local(
@@ -364,8 +394,7 @@
     slot_rows = CAP * steps_n
     position = lengths[None, :] + jnp.arange(steps_n, dtype=jnp.int32)[:, None]
     cosine, sine = turns(position.reshape(-1), HD)
-    fresh = jnp.transpose(new_kv, (1, 2, 0, 3))
-    fresh = jnp.pad(fresh, ((0, 0), (0, 0), (0, 16 - steps_n), (0, 0)))
+    fresh = new_kv.reshape(all_rows, 2 * HD)
     cuts = 8
     vmem = pl.BlockSpec(memory_space=pltpu.VMEM)
     smem = pl.BlockSpec(memory_space=pltpu.SMEM)
@@ -378,11 +407,11 @@
         functools.partial(layer_kernel, n, ni, chunks),
         out_shape=(
             jax.ShapeDtypeStruct((all_rows, share), bf16),
-            jax.ShapeDtypeStruct((ni, 2 * slot_rows, share // 2), bf16),
+            jax.ShapeDtypeStruct((ni * slot_rows, share), bf16),
             jax.ShapeDtypeStruct(slot_shape, bf16),
         ),
         in_specs=[smem] * 5 + [hbm] * 4 + [vmem] * 3,
-        out_specs=(vmem, hbm, hbm),
+        out_specs=(vmem, vmem, hbm),
         scratch_shapes=[
             pltpu.VMEM((cuts, all_rows, width // cuts), bf16),
             pltpu.VMEM((cuts, width // cuts, columns), bf16),
@@ -396,6 +425,8 @@
             pltpu.VMEM(slot_shape, bf16),
             pltpu.VMEM((ni, slot_rows, all_rows), f32),
             pltpu.VMEM((ni, 2 * slot_rows, share // 2), bf16),
+            pltpu.VMEM((ni, 2 * slot_rows, share // 2), bf16),
+            pltpu.VMEM((2, requests, 16, HD), f32),
             dma((cuts,)), dma((cuts,)), dma, dma((n * chunks,)),
             dma((HALVES * hops,)), dma((HALVES * hops,)), dma((HALVES * hops,)), dma((HALVES * hops,)),
             dma((ni,)), dma((ni,)), dma((ni,)), dma((ni,)), dma((2,)),
@@ -408,8 +439,7 @@
         hidden.reshape(-1, width), query_weight, kv_pool, output_weight, fresh, cosine, sine,
     )
     home = home.reshape(steps_n, requests, -1)
-    arrive = arrive.reshape(ni, 2, CAP, steps_n, -1)
-    arrival = jnp.transpose(arrive, (3, 0, 2, 1, 4)).reshape(steps_n, ni * CAP, -1)
+    arrival = arrive.reshape(steps_n, ni * CAP, -1)
     return (home, arrival, got_pages)
 
 

time: 75.3 us -> 67.6 us (0.90)
  Pallas kernels: 65.6 us -> 56.8 us
  local copies, waits for them, and re-layouts: 7.07 us -> 7.88 us
    pallas_call x1, Pallas kernels: 65.6 us -> 56.8 us  [local(): pl.pallas_call(functools.partial(layer_kernel, n, ni, chunks), out_shape=...]
    unnamed x5 -> x4, local copies, waits for them, and re-layouts: 3.92 us -> 7.79 us
    reshape x2 -> x0, local copies, waits for them, and re-layouts: 2.06 us -> none  [the longest x1 1.17 us: local(): arrive = arrive.reshape(ni, 2, CAP, steps_n, -1)]
where the time goes in v5:
time: 67.6 us; the launch traced here: 67 us
  Pallas kernels  56.8 us (84%)
  local copies, waits for them, and re-layouts  7.88 us (12%)
  other arithmetic  1.74 us (3%)
    pallas_call x1, Pallas kernels, local(): pl.pallas_call(functools.partial(layer_kernel, n, ni, chunks), out_shape=...  56.8 us
    unnamed x4, local copies, waits for them, and re-layouts  7.79 us

profile of v5, /device:TPU:0, one launch (start us, length us, event | category | flops | bytes accessed | tf_op | source)
XLA Modules:
  0.0 67.0 jit_solution(3230385945678711568)
XLA Ops:
  0.6 0.7 add_convert_fusion
  1.3 0.1 convert_element_type.11
  1.4 1.5 %copy.15 = bf16[16,8,2,128]{3,1,2,0:T(8,128)(2,1)} copy(bf16[16,8,2,128]{3,2,1,0:T(2,128)(2,1)} %bitcast.14) | data formatting | bytes 131072
  2.9 0.3 fusion
  3.2 0.8 %pad_maximum_fusion = (f32[128,128]{1,0:T(8,128)}, f32[128,128]{1,0:T(8,128)}) fusion(f32[128,64]{1,0:T(8,128)S(1)} %get-tuple-element.11, f32[128,64]{1,0:T(8,128)S(1)} %get-tuple-element.10, f32[128,64]{1,0:T(8,128)S(1)} %get-tuple-element.9), kind=kLoop, calls=%fused_computation.3 | loop fusion | flops 32768 | bytes 229376 | tf_op jit(solution)/shard_map/concatenate | solution.py:26
  3.9 56.8 %shard_map.121 = (bf16[128,2048]{1,0:T(8,128)(2,1)}, bf16[64,2048]{1,0:T(8,128)(2,1)}, bf16[16,3,2,64,128]{4,3,2,1,0:T(8,128)(2,1)}) custom-call(s32[32]{0:T(128)} %lengths.1, s32[3,32]{1,0:T(4,128)} %bitcast.15, s32[8]{0:T(128)} %mig_req.1, s32[8]{0:T(128)} %bitcast.16, s32[8]{0:T(128)} %resume.1, bf16[128,8192]{1,0:T(8,128)(2,1)} %bitcast.10, ...), custom_call_target="tpu_custom_call" | custom-call | tf_op jit(solution)/shard_map/pallas_call | solution.py:406
  60.7 1.9 %copy.19 = bf16[4,32,2048]{2,1,0:T(8,128)(2,1)} copy(bf16[4,32,2048]{2,1,0:T(8,128)(2,1)} %bitcast.11) | data formatting | bytes 1048576
  62.6 1.7 %copy.20 = bf16[4,16,2048]{2,1,0:T(8,128)(2,1)} copy(bf16[4,16,2048]{2,1,0:T(8,128)(2,1)} %bitcast.13) | data formatting | bytes 524288
  64.3 2.8 %copy.21 = bf16[16,3,2,64,128]{4,3,2,1,0:T(8,128)(2,1)} copy(bf16[16,3,2,64,128]{4,3,2,1,0:T(8,128)(2,1)} %get-tuple-element.19) | data formatting | bytes 3145728
  (1 shorter events, 0.0 us)

commit v6 on v5

--- a/solution.py
+++ b/solution.py
@@ -19,11 +19,38 @@
 
 def turns(position, depth):
     half = depth // 2
-    inverse = ROPE_BASE ** (-jnp.arange(half, dtype=jnp.float32) * 2.0 / depth)
+    index = jnp.arange(depth, dtype=jnp.int32)
+    inverse = ROPE_BASE ** (-(index % half).astype(jnp.float32) * 2.0 / depth)
     angles = position.astype(jnp.float32)[:, None] * inverse
-    cosine = jnp.cos(angles)
-    sine = jnp.sin(angles)
-    return jnp.concatenate([cosine, cosine], axis=1), jnp.concatenate([-sine, sine], axis=1)
+    sign = jnp.where(index < half, -1.0, 1.0).astype(jnp.float32)
+    return jnp.cos(angles), jnp.sin(angles) * sign
+
+
+def emit_kernel(*refs):
+    count = (len(refs) - 1) // 2
+    sems = refs[-1]
+    copies = []
+    for source, target in zip(refs[:count], refs[count:2 * count]):
+        for k in range(source.shape[0]):
+            copies.append(
+                pltpu.make_async_copy(source.at[k], target.at[k], sems.at[len(copies)])
+            )
+    for copy in copies:
+        copy.start()
+    for copy in copies:
+        copy.wait()
+
+
+def emit(*arrays):
+    hbm = pl.BlockSpec(memory_space=pl.ANY)
+    return pl.pallas_call(
+        emit_kernel,
+        out_shape=tuple(jax.ShapeDtypeStruct(x.shape, x.dtype) for x in arrays),
+        in_specs=[hbm] * len(arrays),
+        out_specs=(hbm,) * len(arrays),
+        scratch_shapes=[pltpu.SemaphoreType.DMA((sum(x.shape[0] for x in arrays),))],
+        compiler_params=pltpu.CompilerParams(vmem_limit_bytes=60 * 1024 * 1024),
+    )(*arrays)
 
 
 def layer_kernel(
@@ -70,12 +97,10 @@
         )
 
     pool_copy = pltpu.make_async_copy(pool_ref, pool, pool_sem)
-    pool_copy.start()
     for k in range(cuts):
         h_copy(k).start()
         wq_copy(k).start()
-    for k in range(n * chunks):
-        wo_copy(k).start()
+    pool_copy.start()
 
     barrier = pltpu.get_barrier_semaphore()
     for k in range(1, ni):
@@ -98,8 +123,6 @@
     slot_step = slot_row % steps_n
     row_request = (row // rows) * some + row % some
     row_step = (row % rows) // some
-
-    pool_copy.wait()
 
     def fill(d, carry):
         count = jnp.int32(0)
@@ -124,10 +147,6 @@
         select[d] = hit.astype(jnp.float32)
         return carry
 
-    lax.fori_loop(0, ni, fill, 0)
-
-    pl.semaphore_wait(barrier, ni - 1 + (z > 0).astype(jnp.int32) + (z < n - 1).astype(jnp.int32))
-
     def page_copy(k):
         to = lax.rem(me + k, ni)
         return pltpu.make_async_remote_copy(
@@ -146,6 +165,9 @@
     for k in range(cuts):
         h_copy(k).wait()
         wq_copy(k).wait()
+        if k == cuts - 2:
+            for c in range(n * chunks):
+                wo_copy(c).start()
         total = total + jnp.dot(h_buf[k], wq_buf[k], preferred_element_type=jnp.float32)
     for g in range(groups):
         head = total[:, g * hd:(g + 1) * hd]
@@ -153,6 +175,8 @@
         for s in range(steps_n):
             query[:, s * groups + g, :] = head[s * requests:(s + 1) * requests]
 
+    pl.semaphore_wait(barrier, ni - 1 + (z > 0).astype(jnp.int32) + (z < n - 1).astype(jnp.int32))
+
     fresh[...] = jnp.zeros_like(fresh)
     for u in range(steps_n):
         for kind in range(2):
@@ -160,6 +184,7 @@
                 u * requests:(u + 1) * requests, kind * hd:(kind + 1) * hd
             ].astype(jnp.float32)
 
+    pool_copy.wait()
     batch = 8
     old = maxp * page
     span = old + page
@@ -243,6 +268,7 @@
 
         lax.fori_loop(0, n * chunks, compute, 0)
         if h == 0:
+            lax.fori_loop(0, ni, fill, 0)
             for k in range(1, ni):
                 page_copy(k).start()
             own_pages.start()
@@ -440,7 +466,7 @@
     )
     home = home.reshape(steps_n, requests, -1)
     arrival = arrive.reshape(steps_n, ni * CAP, -1)
-    return (home, arrival, got_pages)
+    return emit(home, arrival, got_pages)
 
 
 def solution(mesh):

time: 67.6 us -> 130 us (1.92)
  Pallas kernels: 56.8 us -> 126 us
  local copies, waits for them, and re-layouts: 7.88 us -> 1.56 us
    pallas_call x0 -> x1, Pallas kernels: none -> 72.8 us  [emit(): pl.pallas_call(emit_kernel, out_shape=tuple((jax.ShapeDtypeStruct(x.shape...]
    unnamed x4 -> x1, local copies, waits for them, and re-layouts: 7.79 us -> 1.48 us
    pallas_call x1, Pallas kernels: 56.8 us -> 53 us  [local(): pl.pallas_call(functools.partial(layer_kernel, n, ni, chunks), out_shape=...]
where the time goes in v6:
time: 130 us
  Pallas kernels  126 us (97%)
  other arithmetic  1.64 us (1%)
  local copies, waits for them, and re-layouts  1.56 us (1%)
    pallas_call x1, Pallas kernels, emit(): pl.pallas_call(emit_kernel, out_shape=tuple((jax.ShapeDtypeStruct(x.shape...  72.8 us
    pallas_call x1, Pallas kernels, local(): pl.pallas_call(functools.partial(layer_kernel, n, ni, chunks), out_shape=...  53 us

profile of v6, /device:TPU:0, one launch (start us, length us, event | category | flops | bytes accessed | tf_op | source)
XLA Modules:
  0.0 129.6 jit_solution(2293457278290751367)
XLA Ops:
  0.6 0.7 add_convert_fusion
  1.3 0.1 convert_element_type.18
  1.4 1.5 %copy.15 = bf16[16,8,2,128]{3,1,2,0:T(8,128)(2,1)} copy(bf16[16,8,2,128]{3,2,1,0:T(2,128)(2,1)} %bitcast.14) | data formatting | bytes 131072
  2.9 1.0 fusion
  3.8 53.0 %shard_map.121 = (bf16[128,2048]{1,0:T(8,128)(2,1)}, bf16[64,2048]{1,0:T(8,128)(2,1)}, bf16[16,3,2,64,128]{4,3,2,1,0:T(8,128)(2,1)}) custom-call(s32[32]{0:T(128)} %lengths.1, s32[3,32]{1,0:T(4,128)} %bitcast.15, s32[8]{0:T(128)} %mig_req.1, s32[8]{0:T(128)} %bitcast.16, s32[8]{0:T(128)} %resume.1, bf16[128,8192]{1,0:T(8,128)(2,1)} %bitcast.10, ...), custom_call_target="tpu_custom_call" | custom-call | tf_op jit(solution)/shard_map/pallas_call | solution.py:432
  56.8 72.8 %shard_map.122 = (bf16[4,32,2048]{2,1,0:T(8,128)(2,1)}, bf16[4,16,2048]{2,1,0:T(8,128)(2,1)}, bf16[16,3,2,64,128]{4,3,2,1,0:T(8,128)(2,1)}) custom-call(bf16[4,32,2048]{2,1,0:T(8,128)(2,1)} %bitcast.11, bf16[4,16,2048]{2,1,0:T(8,128)(2,1)} %bitcast.13, bf16[16,3,2,64,128]{4,3,2,1,0:T(8,128)(2,1)} %get-tuple-element.8.refs_2_), custom_call_target="tpu_custom_call" | custom-call | tf_op jit(solution)/shard_map/pallas_call | solution.py:46
  (1 shorter events, 0.0 us)

commit v7 on v6

--- a/solution.py
+++ b/solution.py
@@ -26,29 +26,34 @@
     return jnp.cos(angles), jnp.sin(angles) * sign
 
 
-def emit_kernel(*refs):
-    count = (len(refs) - 1) // 2
-    sems = refs[-1]
-    copies = []
-    for source, target in zip(refs[:count], refs[count:2 * count]):
+def emit_kernel(count, *refs):
+    sources, targets = refs[:count], refs[count:2 * count]
+    buffers = refs[2 * count:3 * count]
+    in_sems, out_sems = refs[3 * count:]
+    ins, outs = [], []
+    for source, buffer, target in zip(sources, buffers, targets):
         for k in range(source.shape[0]):
-            copies.append(
-                pltpu.make_async_copy(source.at[k], target.at[k], sems.at[len(copies)])
-            )
-    for copy in copies:
+            ins.append(pltpu.make_async_copy(source.at[k], buffer.at[k], in_sems.at[len(ins)]))
+            outs.append(pltpu.make_async_copy(buffer.at[k], target.at[k], out_sems.at[len(outs)]))
+    for copy in ins:
         copy.start()
-    for copy in copies:
+    for first, second in zip(ins, outs):
+        first.wait()
+        second.start()
+    for copy in outs:
         copy.wait()
 
 
 def emit(*arrays):
     hbm = pl.BlockSpec(memory_space=pl.ANY)
+    pieces = sum(x.shape[0] for x in arrays)
     return pl.pallas_call(
-        emit_kernel,
+        functools.partial(emit_kernel, len(arrays)),
         out_shape=tuple(jax.ShapeDtypeStruct(x.shape, x.dtype) for x in arrays),
         in_specs=[hbm] * len(arrays),
         out_specs=(hbm,) * len(arrays),
-        scratch_shapes=[pltpu.SemaphoreType.DMA((sum(x.shape[0] for x in arrays),))],
+        scratch_shapes=[pltpu.VMEM(x.shape, x.dtype) for x in arrays]
+        + [pltpu.SemaphoreType.DMA((pieces,)), pltpu.SemaphoreType.DMA((pieces,))],
         compiler_params=pltpu.CompilerParams(vmem_limit_bytes=60 * 1024 * 1024),
     )(*arrays)
 
@@ -273,47 +278,6 @@
                 page_copy(k).start()
             own_pages.start()
 
-    up_lag = jnp.maximum(z - 1, 0)
-    down_lag = jnp.maximum(n - 2 - z, 0)
-    for h in range(HALVES):
-
-        def relay(j, carry, h=h):
-            ju = j - up_lag
-            jd = j - down_lag
-
-            @pl.when((z > 0) & (ju >= 0) & (ju < (n - z) * chunks))
-            def _():
-                up_copy(h * hops + ju).wait_recv()
-                spot = (n - 1 - ju // chunks) * chunks + ju % chunks
-                value = part[h, spot] + up_in[h * hops + ju].astype(jnp.float32)
-
-                @pl.when(ju < (n - 1 - z) * chunks)
-                def _():
-                    up_out[h * hops + ju] = value.astype(jnp.bfloat16)
-                    up_copy(h * hops + ju).start()
-
-                @pl.when(ju >= (n - 1 - z) * chunks)
-                def _():
-                    part[h, spot] = value
-
-            @pl.when((z < n - 1) & (jd >= 0) & (jd < (z + 1) * chunks))
-            def _():
-                down_copy(h * hops + jd).wait_recv()
-                value = part[h, jd] + down_in[h * hops + jd].astype(jnp.float32)
-
-                @pl.when(jd < z * chunks)
-                def _():
-                    down_out[h * hops + jd] = value.astype(jnp.bfloat16)
-                    down_copy(h * hops + jd).start()
-
-                @pl.when(jd >= z * chunks)
-                def _():
-                    part[h, jd] = value
-
-            return carry
-
-        lax.fori_loop(0, hops + n - 2, relay, 0)
-
     selection = select[...].reshape(ni * slot_rows, HALVES * rows).astype(jnp.bfloat16)
     lane_row = lax.broadcasted_iota(jnp.int32, (rows, hd), 0)
     half = chunks // 2
@@ -324,6 +288,47 @@
             gone = (lane_row % some + h * some == mig_req[k]) & (lane_row // some >= resume[k])
             kept = jnp.where(gone, 0, kept)
         stays.append(jnp.concatenate([kept] * (width // hd), axis=1))
+    up_lag = jnp.maximum(z - 1, 0)
+    down_lag = jnp.maximum(n - 2 - z, 0)
+    for h in range(HALVES):
+
+        def relay(j, carry, h=h):
+            ju = j - up_lag
+            jd = j - down_lag
+
+            @pl.when((z > 0) & (ju >= 0) & (ju < (n - z) * chunks))
+            def _():
+                up_copy(h * hops + ju).wait_recv()
+                spot = (n - 1 - ju // chunks) * chunks + ju % chunks
+                value = part[h, spot] + up_in[h * hops + ju].astype(jnp.float32)
+
+                @pl.when(ju < (n - 1 - z) * chunks)
+                def _():
+                    up_out[h * hops + ju] = value.astype(jnp.bfloat16)
+                    up_copy(h * hops + ju).start()
+
+                @pl.when(ju >= (n - 1 - z) * chunks)
+                def _():
+                    part[h, spot] = value
+
+            @pl.when((z < n - 1) & (jd >= 0) & (jd < (z + 1) * chunks))
+            def _():
+                down_copy(h * hops + jd).wait_recv()
+                value = part[h, jd] + down_in[h * hops + jd].astype(jnp.float32)
+
+                @pl.when(jd < z * chunks)
+                def _():
+                    down_out[h * hops + jd] = value.astype(jnp.bfloat16)
+                    down_copy(h * hops + jd).start()
+
+                @pl.when(jd >= z * chunks)
+                def _():
+                    part[h, jd] = value
+
+            return carry
+
+        lax.fori_loop(0, hops + n - 2, relay, 0)
+
     for c in range(half):
         pieces = []
         for d in (c, c + half):

time: 130 us -> 59.8 us (0.46)
  Pallas kernels: 126 us -> 55.7 us
    pallas_call x1, Pallas kernels: 72.8 us -> 2.78 us  [emit(): pl.pallas_call(functools.partial(emit_kernel, len(arrays)), out_shape=tup...]
where the time goes in v7:
time: 59.8 us; the launch traced here: 59.5 us
  Pallas kernels  55.7 us (93%)
  other arithmetic  1.64 us (3%)
  local copies, waits for them, and re-layouts  1.56 us (3%)
  between operations  0.65 us (1%)
    pallas_call x1, Pallas kernels, local(): pl.pallas_call(functools.partial(layer_kernel, n, ni, chunks), out_shape=...  52.9 us
    pallas_call x1, Pallas kernels, emit(): pl.pallas_call(functools.partial(emit_kernel, len(arrays)), out_shape=tup...  2.78 us
    unnamed x1, local copies, waits for them, and re-layouts  1.48 us

profile of v7, /device:TPU:0, one launch (start us, length us, event | category | flops | bytes accessed | tf_op | source)
XLA Modules:
  0.0 59.5 jit_solution(5503919467900829012)
XLA Ops:
  0.6 0.7 %add_convert_fusion = f32[4,32]{1,0:T(4,128)S(1)} fusion(s32[32]{0:T(128)} %lengths.1), kind=kLoop, calls=%fused_computation.4 | loop fusion | flops 256 | bytes 640 | tf_op jit(solution)/shard_map/convert_element_type | solution.py:24
  1.3 0.1 convert_element_type.18
  1.4 1.5 %copy.15 = bf16[16,8,2,128]{3,1,2,0:T(8,128)(2,1)} copy(bf16[16,8,2,128]{3,2,1,0:T(2,128)(2,1)} %bitcast.14) | data formatting | bytes 131072
  2.9 1.0 %fusion = (f32[128,128]{1,0:T(8,128)}, f32[128,128]{1,0:T(8,128)}) fusion(f32[128]{0:T(128)S(1)} %get-tuple-element.11, f32[128]{0:T(128)S(1)} %get-tuple-element.12, f32[128]{0:T(128)S(1)} %convert_element_type.18), kind=kLoop, calls=%fused_computation.2 | loop fusion | flops 32768 | bytes 132608 | tf_op jit(solution)/shard_map/mul | solution.py:26
  3.8 52.9 %shard_map.121 = (bf16[128,2048]{1,0:T(8,128)(2,1)}, bf16[64,2048]{1,0:T(8,128)(2,1)}, bf16[16,3,2,64,128]{4,3,2,1,0:T(8,128)(2,1)}) custom-call(s32[32]{0:T(128)} %lengths.1, s32[3,32]{1,0:T(4,128)} %bitcast.15, s32[8]{0:T(128)} %mig_req.1, s32[8]{0:T(128)} %bitcast.16, s32[8]{0:T(128)} %resume.1, bf16[128,8192]{1,0:T(8,128)(2,1)} %bitcast.10, ...), custom_call_target="tpu_custom_call" | custom-call | tf_op jit(solution)/shard_map/pallas_call | solution.py:437
  56.7 2.8 %shard_map.122 = (bf16[4,32,2048]{2,1,0:T(8,128)(2,1)}, bf16[4,16,2048]{2,1,0:T(8,128)(2,1)}, bf16[16,3,2,64,128]{4,3,2,1,0:T(8,128)(2,1)}) custom-call(bf16[4,32,2048]{2,1,0:T(8,128)(2,1)} %bitcast.11, bf16[4,16,2048]{2,1,0:T(8,128)(2,1)} %bitcast.13, bf16[16,3,2,64,128]{4,3,2,1,0:T(8,128)(2,1)} %get-tuple-element.8.refs_2_), custom_call_target="tpu_custom_call" | custom-call | tf_op jit(solution)/shard_map/pallas_call | solution.py:50
  (1 shorter events, 0.0 us)

commit v8 on v7

--- a/solution.py
+++ b/solution.py
@@ -9,7 +9,7 @@
 
 HD = 128
 CAP = 2
-HALVES = 2
+HALVES = 1
 
 
 ROPE_BASE = 500000.0
@@ -419,7 +419,7 @@
     all_rows = steps_n * requests
     rows = all_rows // HALVES
     share = output_weight.shape[1] // n
-    chunk = min(1024, share // 2)
+    chunk = min(512, share // 2)
     chunks = share // chunk
     hops = (n - 1) * chunks
     slot_rows = CAP * steps_n

time: 59.8 us -> 59 us (0.987)
  the two profiles are of different devices: /device:TPU:0 before, /device:TPU:17 now
where the time goes in v8:
time: 59 us; the launch traced here: 58.7 us
  Pallas kernels  54.9 us (93%)
  other arithmetic  1.64 us (3%)
  local copies, waits for them, and re-layouts  1.56 us (3%)
  between operations  0.65 us (1%)
    pallas_call x1, Pallas kernels, local(): pl.pallas_call(functools.partial(layer_kernel, n, ni, chunks), out_shape=...  52.1 us
    pallas_call x1, Pallas kernels, emit(): pl.pallas_call(functools.partial(emit_kernel, len(arrays)), out_shape=tup...  2.78 us
    unnamed x1, local copies, waits for them, and re-layouts  1.48 us

profile of v8, /device:TPU:17, one launch (start us, length us, event | category | flops | bytes accessed | tf_op | source)
XLA Modules:
  0.0 58.7 jit_solution(12915048193679505096)
XLA Ops:
  0.6 0.7 %add_convert_fusion = f32[4,32]{1,0:T(4,128)S(1)} fusion(s32[32]{0:T(128)} %lengths.1), kind=kLoop, calls=%fused_computation.4 | loop fusion | flops 256 | bytes 640 | tf_op jit(solution)/shard_map/convert_element_type | solution.py:24
  1.3 0.1 convert_element_type.18
  1.4 1.5 %copy.15 = bf16[16,8,2,128]{3,1,2,0:T(8,128)(2,1)} copy(bf16[16,8,2,128]{3,2,1,0:T(2,128)(2,1)} %bitcast.14) | data formatting | bytes 131072
  2.9 1.0 %fusion = (f32[128,128]{1,0:T(8,128)}, f32[128,128]{1,0:T(8,128)}) fusion(f32[128]{0:T(128)S(1)} %get-tuple-element.11, f32[128]{0:T(128)S(1)} %get-tuple-element.12, f32[128]{0:T(128)S(1)} %convert_element_type.18), kind=kLoop, calls=%fused_computation.2 | loop fusion | flops 32768 | bytes 132608 | tf_op jit(solution)/shard_map/mul | solution.py:26
  3.8 52.1 %shard_map.121 = (bf16[128,2048]{1,0:T(8,128)(2,1)}, bf16[64,2048]{1,0:T(8,128)(2,1)}, bf16[16,3,2,64,128]{4,3,2,1,0:T(8,128)(2,1)}) custom-call(s32[32]{0:T(128)} %lengths.1, s32[3,32]{1,0:T(4,128)} %bitcast.15, s32[8]{0:T(128)} %mig_req.1, s32[8]{0:T(128)} %bitcast.16, s32[8]{0:T(128)} %resume.1, bf16[128,8192]{1,0:T(8,128)(2,1)} %bitcast.10, ...), custom_call_target="tpu_custom_call" | custom-call | tf_op jit(solution)/shard_map/pallas_call | solution.py:437
  55.9 2.8 %shard_map.122 = (bf16[4,32,2048]{2,1,0:T(8,128)(2,1)}, bf16[4,16,2048]{2,1,0:T(8,128)(2,1)}, bf16[16,3,2,64,128]{4,3,2,1,0:T(8,128)(2,1)}) custom-call(bf16[4,32,2048]{2,1,0:T(8,128)(2,1)} %bitcast.11, bf16[4,16,2048]{2,1,0:T(8,128)(2,1)} %bitcast.13, bf16[16,3,2,64,128]{4,3,2,1,0:T(8,128)(2,1)} %get-tuple-element.8.refs_2_), custom_call_target="tpu_custom_call" | custom-call | tf_op jit(solution)/shard_map/pallas_call | solution.py:50
  (1 shorter events, 0.0 us)
